TPU v7x, 512 devices: a whole 4x4x16 slice. The times are simulated.
512 devices in a mesh: dp: 16 (over x, z_hi, core), ctx: 32 (over z_lo, y).
Axes of the slice: x: 4, y: 4, z: 16 (z_hi: 2, z_lo: 8; z = z_hi * 8 + z_lo), core: 2. Of those that a mesh axis runs over, the one named last changes fastest.
Arguments:
- queries: bfloat16 [16, 12288, 1536], P('dp', 'ctx'), may hold values from -160 to 160
- key_rows: bfloat16 [16, 12288, 1536], P('dp', 'ctx'), may hold values from -8 to 8
- value_rows: bfloat16 [16, 12288, 1536], P('dp', 'ctx'), may hold values from -6 to 6
- tile_lists: int32 [16, 32, 5], P('dp', 'ctx'), may hold values from 0 to 31, as said below
- tile_counts: int32 [16, 32], P('dp', 'ctx'), may hold values from 1 to 5
- out_weight: bfloat16 [1536, 1536], P('dp'), may hold values from -0.15625 to 0.15625
Outputs:
- projected: bfloat16 [16, 12288, 1536], P('dp', 'ctx')
Inputs may be any that keep to these rules, and one draw needn't show every extreme that they name: For s < tile_counts[b, t], tile_lists[b, t, s] are distinct tiles of the video within 2 of t, increasing, and t is among them; later slots hold t.
All inputs are finite; a program needn't handle non-finite values.
Results may differ from a plain program's by a relative error of at most 0.0056.
Values may be sent and summed in bfloat16 or wider, within the bound.
No kernel may reach another device: no remote copies, remote signals or barrier semaphores. Data moves between devices by JAX's collectives and lax.ppermute only.
A program may use at most 64 MiB of HBM per device.

v0:
```python
import math

import jax
import jax.numpy as jnp
from jax import lax
from jax.sharding import PartitionSpec as P

HEADS = 12
HD = 128
DOUT = 1536
REACH = 2
SLOTS = 5


def from_behind(value, axis, by):
    size = lax.axis_size(axis)
    pairs = [(i, i + by) for i in range(size) if 0 <= i + by < size]
    return lax.ppermute(value, axis, pairs)


def masked_video(query_block, key_window, value_window, visible_tiles):
    tok_rows = query_block.shape[0]
    expanded = (jnp.repeat(visible_tiles, tok_rows) > 0)[None, :]

    def per_head(head_pos):
        start_col = head_pos * HD
        query_head = lax.dynamic_slice_in_dim(query_block, start_col, HD, 1)
        key_head = lax.dynamic_slice_in_dim(key_window, start_col, HD, 1)
        value_head = lax.dynamic_slice_in_dim(value_window, start_col, HD, 1)
        scores = jnp.einsum(
            "td,kd->tk", query_head, key_head, preferred_element_type=jnp.float32
        ) * (1.0 / math.sqrt(HD))
        peak_rows = jnp.max(jnp.where(expanded, scores, jnp.float32(-1e30)), axis=1, keepdims=True)
        exponent = jnp.where(expanded, jnp.exp(scores - peak_rows), jnp.float32(0.0))
        totals = jnp.sum(exponent, axis=1, keepdims=True)
        mixture = jnp.dot(
            exponent.astype(jnp.bfloat16), value_head, preferred_element_type=jnp.float32
        )
        return (mixture / totals).astype(jnp.bfloat16)

    per_heads = lax.map(per_head, jnp.arange(HEADS, dtype=jnp.int32))
    return per_heads.transpose(1, 0, 2).reshape(tok_rows, HEADS * HD)


def per_device(queries, key_rows, value_rows, tile_lists, tile_counts, out_weight):
    videos = queries.shape[0]
    tok_rows = queries.shape[1]
    channels = queries.shape[2]
    tile_here = lax.axis_index("ctx")
    key_value = jnp.stack([key_rows, value_rows])
    below_parts = [from_behind(key_value, "ctx", distance) for distance in range(REACH, 0, -1)]
    above_parts = [from_behind(key_value, "ctx", -distance) for distance in range(1, REACH + 1)]
    windowed = jnp.concatenate(below_parts + [key_value] + above_parts, axis=2)
    offsets = jnp.arange(SLOTS, dtype=jnp.int32) - REACH
    in_use = jnp.arange(SLOTS, dtype=jnp.int32)[None, :] < tile_counts[:, 0][:, None]
    matches = (tile_lists[:, 0, :, None] == (tile_here + offsets)[None, None, :]) & in_use[
        :, :, None
    ]
    visible = jnp.any(matches, axis=1).astype(jnp.int32)
    attended = [masked_video(queries[0], windowed[0, 0], windowed[1, 0], visible[0])]
    attention = jnp.stack(attended).reshape(videos * tok_rows, channels)
    projected = jnp.dot(
        attention,
        lax.all_gather(out_weight, "dp", axis=0, tiled=True),
        preferred_element_type=jnp.float32,
    )
    return projected.astype(jnp.bfloat16).reshape(videos, tok_rows, DOUT)


def solution(mesh):
    in_specs = (
        P("dp", "ctx", None),
        P("dp", "ctx", None),
        P("dp", "ctx", None),
        P("dp", "ctx", None),
        P("dp", "ctx"),
        P("dp", None),
    )
    out_specs = P("dp", "ctx", None)
    return jax.shard_map(
        per_device, mesh=mesh, in_specs=in_specs, out_specs=out_specs, check_vma=False
    )
```

profile of v0, /device:TPU:406, one launch (start us, length us, event | category | flops | bytes accessed | tf_op | source)
XLA Modules:
  0.0 305.7 jit_solution(16423190190118336372)
XLA Ops:
  6.5 1.9 pad_maximum_fusion
  8.4 2.7 collective-permute-start
  11.1 4.1 %collective-permute-start.1 = (bf16[2,1,384,1536]{3,2,1,0:T(8,128)(2,1)S(1)}, bf16[2,1,384,1536]{3,2,1,0:T(8,128)(2,1)}, u32[]{:S(2)}, u32[]{:S(2)}) collective-permute-start(bf16[2,1,384,1536]{3,2,1,0:T(8,128)(2,1)S(1)} %pad_maximum_fusion), channel_id=1, source_target_pairs={{0,1},{1,2},{2,3},{3,4},{4,5},{5,6},{6,7},{7,8},{8,9},{9,10},{10,1... | collective-permute-start | bytes 7077896 | tf_op jit(solution)/shard_map/ppermute | solution.py:18
  15.2 1.9 collective-permute-start.2
  17.1 7.8 %collective-permute-start.3 = (bf16[2,1,384,1536]{3,2,1,0:T(8,128)(2,1)S(1)}, bf16[2,1,384,1536]{3,2,1,0:T(8,128)(2,1)}, u32[]{:S(2)}, u32[]{:S(2)}) collective-permute-start(bf16[2,1,384,1536]{3,2,1,0:T(8,128)(2,1)S(1)} %pad_maximum_fusion), channel_id=1, source_target_pairs={{2,0},{3,1},{4,2},{5,3},{6,4},{7,5},{8,6},{9,7},{10,8},{11,9},{12,... | collective-permute-start | bytes 7077896 | tf_op jit(solution)/shard_map/ppermute | solution.py:18
  25.8 48.5 %collective-permute-done = bf16[2,1,384,1536]{3,2,1,0:T(8,128)(2,1)} collective-permute-done((bf16[2,1,384,1536]{3,2,1,0:T(8,128)(2,1)S(1)}, bf16[2,1,384,1536]{3,2,1,0:T(8,128)(2,1)}, u32[]{:S(2)}, u32[]{:S(2)}) %collective-permute-start) | collective-permute-done | bytes 2359328 | tf_op jit(solution)/shard_map/ppermute | solution.py:18
  74.3 1.8 constant_dynamic-update-slice_fusion.5
  76.1 39.3 %collective-permute-done.1 = bf16[2,1,384,1536]{3,2,1,0:T(8,128)(2,1)} collective-permute-done((bf16[2,1,384,1536]{3,2,1,0:T(8,128)(2,1)S(1)}, bf16[2,1,384,1536]{3,2,1,0:T(8,128)(2,1)}, u32[]{:S(2)}, u32[]{:S(2)}) %collective-permute-start.1) | collective-permute-done | bytes 2359328 | tf_op jit(solution)/shard_map/ppermute | solution.py:18
  115.4 1.8 constant_dynamic-update-slice_fusion.4
  117.5 1.8 constant_dynamic-update-slice_fusion.2
  119.3 101.1 %collective-permute-done.3 = bf16[2,1,384,1536]{3,2,1,0:T(8,128)(2,1)} collective-permute-done((bf16[2,1,384,1536]{3,2,1,0:T(8,128)(2,1)S(1)}, bf16[2,1,384,1536]{3,2,1,0:T(8,128)(2,1)}, u32[]{:S(2)}, u32[]{:S(2)}) %collective-permute-start.3) | collective-permute-done | bytes 2359328 | tf_op jit(solution)/shard_map/ppermute | solution.py:18
  220.4 1.8 constant_dynamic-update-slice_fusion.1
  222.2 4.7 %slice_bitcast_fusion = (bf16[1920,1536]{1,0:T(8,128)(2,1)}, bf16[1920,1536]{1,0:T(8,128)(2,1)}) fusion(bf16[2,1,1920,1536]{3,2,1,0:T(8,128)(2,1)S(1)} %constant_dynamic-update-slice_fusion.1), kind=kLoop, calls=%fused_computation.20 | loop fusion | bytes 23592960 | tf_op jit(solution)/shard_map/squeeze | solution.py:60
  227.0 66.5 %while.11 = (s32[]{:T(128)}, bf16[12,384,128]{1,2,0:T(8,128)(2,1)S(1)}, s32[12]{0:T(128)S(1)}, bf16[384,1536]{1,0:T(8,128)(2,1)}, bf16[1920,1536]{1,0:T(8,128)(2...) while((s32[]{:T(128)}, ...), condition=%wide.region_4.5_spmd.clone, body=%wide.region_1.4_spmd.clone.sunk | while | flops 384220416 | bytes 10440628 | solution.py:41
  228.3 1.8 select_reduce_fusion.2
  230.1 0.6 fusion.33
  230.7 1.6 fusion.34
  233.8 1.8 select_reduce_fusion.2
  235.6 0.6 fusion.33
  236.2 1.6 fusion.34
  239.4 1.8 select_reduce_fusion.2
  241.1 0.6 fusion.33
  241.8 1.6 fusion.34
  244.9 1.8 select_reduce_fusion.2
  246.7 0.6 fusion.33
  247.3 1.6 fusion.34
  250.5 1.8 select_reduce_fusion.2
  252.9 1.6 fusion.34
  256.0 1.8 select_reduce_fusion.2
  257.8 0.6 fusion.33
  258.4 1.6 fusion.34
  261.5 1.8 select_reduce_fusion.2
  263.3 0.6 fusion.33
  263.9 1.6 fusion.34
  267.1 1.8 select_reduce_fusion.2
  269.5 1.6 fusion.34
  272.6 1.8 select_reduce_fusion.2
  274.4 0.6 fusion.33
  275.0 1.6 fusion.34
  278.2 1.8 select_reduce_fusion.2
  279.9 0.6 fusion.33
  280.6 1.6 fusion.34
  283.7 1.8 select_reduce_fusion.2
  286.1 1.6 fusion.34
  289.2 1.8 select_reduce_fusion.2
  291.0 0.6 fusion.33
  291.6 1.6 fusion.34
  293.5 5.4 %fusion.24 = bf16[1,384,1536]{2,1,0:T(8,128)(2,1)} fusion(bf16[384,1536]{0,1:T(8,128)(2,1)S(1)} %bitcast.30, bf16[1536,1536]{1,0:T(8,128)(2,1)} %all-gather.2.cloned.1.call-done), kind=kOutput, calls=%fused_computation.23 | convolution fusion | flops 1812529152 | bytes 7077888 | tf_op jit(solution)/shard_map/dot_general | solution.py:62
  (80 shorter events, 12.4 us)
Async XLA Ops:
  6.5 19.1 %copy-start.2 = (s32[1,1,5]{2,1,0:T(1,128)S(1)}, s32[1,1,5]{2,1,0:T(1,128)}, u32[]{:S(2)}) copy-start(s32[1,1,5]{2,1,0:T(1,128)} %param.11) | copy-start | bytes 64
  6.5 286.9 %all-gather.2.cloned.1.call-start = ((), (), s32[]{:S(2)}) async-start(), calls=%async_computation | async-start | bytes 5013504 | tf_op jit(solution)/shard_map/all_gather | solution.py:64
  8.4 65.9 %collective-permute-start = (bf16[2,1,384,1536]{3,2,1,0:T(8,128)(2,1)S(1)}, bf16[2,1,384,1536]{3,2,1,0:T(8,128)(2,1)}, u32[]{:S(2)}, u32[]{:S(2)}) collective-permute-start(bf16[2,1,384,1536]{3,2,1,0:T(8,128)(2,1)S(1)} %pad_maximum_fusion), channel_id=1, source_target_pairs={{0,2},{1,3},{2,4},{3,5},{4,6},{5,7},{6,8},{7,9},{8,10},{9,11},{10,... | collective-permute-start | bytes 7077896 | tf_op jit(solution)/shard_map/ppermute | solution.py:18
  11.1 104.3 %collective-permute-start.1 = (bf16[2,1,384,1536]{3,2,1,0:T(8,128)(2,1)S(1)}, bf16[2,1,384,1536]{3,2,1,0:T(8,128)(2,1)}, u32[]{:S(2)}, u32[]{:S(2)}) collective-permute-start(bf16[2,1,384,1536]{3,2,1,0:T(8,128)(2,1)S(1)} %pad_maximum_fusion), channel_id=1, source_target_pairs={{0,1},{1,2},{2,3},{3,4},{4,5},{5,6},{6,7},{7,8},{8,9},{9,10},{10,1... | collective-permute-start | bytes 7077896 | tf_op jit(solution)/shard_map/ppermute | solution.py:18
  15.2 102.2 %collective-permute-start.2 = (bf16[2,1,384,1536]{3,2,1,0:T(8,128)(2,1)S(1)}, bf16[2,1,384,1536]{3,2,1,0:T(8,128)(2,1)}, u32[]{:S(2)}, u32[]{:S(2)}) collective-permute-start(bf16[2,1,384,1536]{3,2,1,0:T(8,128)(2,1)S(1)} %pad_maximum_fusion), channel_id=1, source_target_pairs={{1,0},{2,1},{3,2},{4,3},{5,4},{6,5},{7,6},{8,7},{9,8},{10,9},{11,1... | collective-permute-start | bytes 7077896 | tf_op jit(solution)/shard_map/ppermute | solution.py:18
  17.1 203.3 %collective-permute-start.3 = (bf16[2,1,384,1536]{3,2,1,0:T(8,128)(2,1)S(1)}, bf16[2,1,384,1536]{3,2,1,0:T(8,128)(2,1)}, u32[]{:S(2)}, u32[]{:S(2)}) collective-permute-start(bf16[2,1,384,1536]{3,2,1,0:T(8,128)(2,1)S(1)} %pad_maximum_fusion), channel_id=1, source_target_pairs={{2,0},{3,1},{4,2},{5,3},{6,4},{7,5},{8,6},{9,7},{10,8},{11,9},{12,... | collective-permute-start | bytes 7077896 | tf_op jit(solution)/shard_map/ppermute | solution.py:18
  76.1 41.2 %copy-start = (bf16[1,384,1536]{2,1,0:T(8,128)(2,1)S(1)}, bf16[1,384,1536]{2,1,0:T(8,128)(2,1)}, u32[]{:S(2)}) copy-start(bf16[1,384,1536]{2,1,0:T(8,128)(2,1)} %param.10) | copy-start | bytes 3538948
  76.1 41.2 %copy-start.1 = (bf16[1,384,1536]{2,1,0:T(8,128)(2,1)S(1)}, bf16[1,384,1536]{2,1,0:T(8,128)(2,1)}, u32[]{:S(2)}) copy-start(bf16[1,384,1536]{2,1,0:T(8,128)(2,1)} %param.9) | copy-start | bytes 3538948
Sparse Core Ops, SparseCore 0:
  25.1 117.8 all-gather.1
where the time goes:
time: 307 us; the launch traced here: 306 us
  waiting for transfers between devices  189 us (62%)
  matrix products  46.3 us (15%)
  local copies, waits for them, and re-layouts  22.2 us (7%)
  starting transfers between devices  16.5 us (5%)
  between operations  14.2 us (5%)
  other arithmetic  9.69 us (3%)
  loops' own time  7.84 us (3%)
    ppermute x4, waiting for transfers between devices, from_behind(): return lax.ppermute(value, axis, pairs)  189 us
    dot_general x12, matrix products, per_head(): jnp.einsum('td,kd->tk', query_head, key_head, preferred_element_type=jnp....  21.2 us
    dot_general x12, matrix products, per_head(): jnp.dot(exponent.astype(jnp.bfloat16), value_head, preferred_element_type...  19.7 us
    ppermute x4, starting transfers between devices, from_behind(): return lax.ppermute(value, axis, pairs)  16.5 us
    another operation x1, loops' own time, masked_video(): per_heads = lax.map(per_head, jnp.arange(HEADS, dtype=jnp.int32))  7.84 us
    reduce_sum x12, other arithmetic, per_head(): totals = jnp.sum(exponent, axis=1, keepdims=True)  7.57 us
    dynamic_slice x12, local copies, waits for them, and re-layouts, masked_video(): per_heads = lax.map(per_head, jnp.arange(HEADS, dtype=jnp.int32))  7.37 us
  transfers between devices with their start and end apart: 5, of which 3 were waited for; matrix products, arithmetic and copies ran while one was open for 23% of the time, Pallas kernels for 0%

commit v1 on v0

v1 whole, which is shorter than its diff:
```python
import math

import jax
import jax.numpy as jnp
from jax import lax
from jax.experimental import pallas as pl
from jax.experimental.pallas import tpu as pltpu
from jax.sharding import PartitionSpec as P

HD = 128
SLOTS = 5
TILE = 384
DOUT = 1536
RING = 4
RUNS = 8
HEADS_HERE = 3
GC = HEADS_HERE * HD
EXTRA = 16
CHUNKS = ((0, 2), (2, 1))
FACTOR = math.log2(math.e) / math.sqrt(HD)
VMEM = 100 * 1024 * 1024 // 2


def z_pairs(by):
    return [
        (z * RING + y, (z + by) * RING + y)
        for z in range(RUNS)
        for y in range(RING)
        if 0 <= z + by < RUNS
    ]


def mirror_pairs():
    pairs = []
    for x in range(4):
        for high in range(2):
            for core in range(2):
                for z in range(RUNS):
                    for y in range(RING):
                        here = (x * 4 + high * 2 + core) * 32 + z * RING + y
                        there = (x * 4 + (1 - high) * 2 + core) * 32 + (RUNS - 1 - z) * RING + y
                        pairs.append((here, there))
    return pairs


def call(kernel, name, outs, scratch, flops, nbytes, smem):
    any_spec = pl.BlockSpec(memory_space=pl.ANY)

    def run(*args):
        specs = [
            pl.BlockSpec(memory_space=pltpu.SMEM) if i < smem else any_spec
            for i in range(len(args))
        ]
        return pl.pallas_call(
            kernel,
            out_shape=outs,
            in_specs=specs,
            out_specs=jax.tree.map(lambda _: any_spec, outs),
            scratch_shapes=scratch,
            compiler_params=pltpu.CompilerParams(vmem_limit_bytes=VMEM),
            cost_estimate=pl.CostEstimate(flops=flops, bytes_accessed=nbytes, transcendentals=0),
            name=name,
        )(*args)

    return run


def pack_kernel(sources, *refs):
    ins, out, sems = refs[:sources], refs[sources], refs[-1]
    copies = []
    for at in range(RING):
        for i, ref in enumerate(ins):
            copies.append(
                pltpu.make_async_copy(
                    ref.at[0, :, pl.ds(at * GC, GC)],
                    out.at[at, i, pl.ds(0, TILE)],
                    sems.at[len(copies)],
                )
            )
            copies[-1].start()
    for copy in copies:
        copy.wait()


def pack(*arrays):
    count = len(arrays)
    return call(
        lambda *refs: pack_kernel(count, *refs),
        "pack",
        jax.ShapeDtypeStruct((RING, count, TILE, GC), jnp.bfloat16),
        [pltpu.SemaphoreType.DMA((RING * count,))],
        0,
        count * TILE * DOUT * 4,
        0,
    )(*arrays)


def pack_plan_kernel(source, plan, out, sems):
    copies = []
    for at in range(RING):
        for part in (
            (source.at[0, :, pl.ds(at * GC, GC)], out.at[at, pl.ds(0, TILE)]),
            (plan, out.at[at, pl.ds(TILE, EXTRA)]),
        ):
            copies.append(pltpu.make_async_copy(*part, sems.at[len(copies)]))
            copies[-1].start()
    for copy in copies:
        copy.wait()


def pack_plan(array, plan):
    return call(
        pack_plan_kernel,
        "pack_plan",
        jax.ShapeDtypeStruct((RING, TILE + EXTRA, GC), jnp.bfloat16),
        [pltpu.SemaphoreType.DMA((RING * 2,))],
        0,
        TILE * DOUT * 4,
        0,
    )(array, plan)


def attend_kernel(first, heads, lists, *refs):
    q_in, kv_in, before, after, out, qb, kvb, ob, in_sems, out_sems = refs
    wide = heads * HD
    columns = pl.ds(first * HD, wide)
    y = lax.rem(lax.axis_index("ctx"), RING)
    base = lax.axis_index("ctx") - y
    copies = []
    for source, target in (
        (q_in.at[:, pl.ds(0, TILE), columns], qb),
        (kv_in.at[:, :, :, columns], kvb.at[pl.ds(0, 4)]),
        (before.at[:, :, :, columns], kvb.at[pl.ds(4, 2)]),
        (after.at[:, :, :, columns], kvb.at[pl.ds(6, 2)]),
    ):
        copies.append(pltpu.make_async_copy(source, target, in_sems.at[len(copies)]))
        copies[-1].start()
    for copy in copies:
        copy.wait()
    ones = jnp.ones((TILE, HD), jnp.bfloat16)

    def body(step, carry):
        at = lax.rem(step, RING)
        col = pl.ds(pl.multiple_of(lax.div(step, RING) * HD, HD), HD)
        live = lists[at, SLOTS]
        for count in range(1, SLOTS + 1):

            @pl.when(live == count)
            def _():
                slots = []
                for s in range(count):
                    tile = lists[at, s] - base
                    slots.append(tile + jnp.where(tile < 0, 6, jnp.where(tile < RING, 0, 2)))
                query = qb[at, :, col]
                scores = [
                    lax.dot_general(
                        query,
                        kvb[slot, 0, :, col],
                        (((1,), (1,)), ((), ())),
                        preferred_element_type=jnp.float32,
                    )
                    for slot in slots
                ]
                high = scores[0]
                for score in scores[1:]:
                    high = jnp.maximum(high, score)
                peak = jnp.max(high, axis=1, keepdims=True)
                total = jnp.zeros((TILE, 2 * HD), jnp.float32)
                for slot, score in zip(slots, scores):
                    probs = jnp.exp2((score - peak) * FACTOR).astype(jnp.bfloat16)
                    value = jnp.concatenate([kvb[slot, 1, :, col], ones], axis=1)
                    total += jnp.dot(probs, value, preferred_element_type=jnp.float32)
                ob[at, :, col] = (total[:, :HD] / total[:, HD:]).astype(jnp.bfloat16)

        return carry

    lax.fori_loop(0, RING * heads, body, 0)
    last = pltpu.make_async_copy(ob, out, out_sems.at[0])
    last.start()
    last.wait()


def attend(first, heads, lists, *arrays):
    wide = heads * HD
    return call(
        lambda *refs: attend_kernel(first, heads, *refs),
        f"attend{first}",
        jax.ShapeDtypeStruct((RING, TILE, wide), jnp.bfloat16),
        [
            pltpu.VMEM((RING, TILE, wide), jnp.bfloat16),
            pltpu.VMEM((2 * RING, 2, TILE, wide), jnp.bfloat16),
            pltpu.VMEM((RING, TILE, wide), jnp.bfloat16),
            pltpu.SemaphoreType.DMA((4,)),
            pltpu.SemaphoreType.DMA((1,)),
        ],
        heads * 5_000_000_000,
        heads * 1_600_000,
        1,
    )(lists, *arrays)


def project(weight, parts):
    def kernel(*refs):
        ins, (own_in, other_in, out, rows, weights, result, sems) = refs[: len(parts)], refs[len(parts) :]
        high = lax.rem(lax.div(lax.axis_index("dp"), 2), 2)
        copies = []

        def copy(source, target):
            copies.append(pltpu.make_async_copy(source, target, sems.at[len(copies)]))
            copies[-1].start()

        for ref, half in ((own_in, high), (other_in, 1 - high)):
            for pair in range(8):
                place = ((pair // 2) * 4 + half * 2 + pair % 2) * 96
                copy(
                    ref.at[pl.ds(pair * 96, 96)],
                    weights.at[pl.ds(pl.multiple_of(place, 96), 96)],
                )
        for ref, (first, heads) in zip(ins, CHUNKS):
            for g in range(RING):
                copy(ref.at[g], rows.at[:, pl.ds(g * GC + first * HD, heads * HD)])
        for each in copies:
            each.wait()

        def body(step, carry):
            col = pl.ds(pl.multiple_of(step * 512, 512), 512)
            result[:, col] = jnp.dot(
                rows[...], weights[:, col], preferred_element_type=jnp.float32
            ).astype(jnp.bfloat16)
            return carry

        lax.fori_loop(0, DOUT // 512, body, 0)
        last = pltpu.make_async_copy(result, out.at[0], sems.at[len(copies)])
        last.start()
        last.wait()

    return call(
        kernel,
        "project",
        jax.ShapeDtypeStruct((1, TILE, DOUT), jnp.bfloat16),
        [
            pltpu.VMEM((TILE, DOUT), jnp.bfloat16),
            pltpu.VMEM((DOUT, DOUT), jnp.bfloat16),
            pltpu.VMEM((TILE, DOUT), jnp.bfloat16),
            pltpu.SemaphoreType.DMA((16 + RING * len(parts) + 1,)),
        ],
        2 * TILE * DOUT * DOUT,
        8_000_000,
        0,
    )(*parts, *weight)


def per_device(queries, key_rows, value_rows, tile_lists, tile_counts, out_weight):
    groups = [[z * RING + y for y in range(RING)] for z in range(RUNS)]
    fours = [[x * 4 + high * 2 + core for x in range(4) for core in range(2)] for high in range(2)]

    def exchange(value):
        return lax.all_to_all(value, "ctx", 0, 0, axis_index_groups=groups)

    def gather(value):
        return lax.all_gather(value, "dp", axis=0, tiled=True, axis_index_groups=fours)

    kv = pack(key_rows, value_rows)
    other = lax.ppermute(out_weight, ("dp", "ctx"), mirror_pairs())
    weight = gather(out_weight), gather(other)
    plan = jnp.concatenate([tile_lists[0], tile_counts], axis=1).astype(jnp.bfloat16)
    plan = jnp.pad(plan, ((0, EXTRA - 1), (0, GC - SLOTS - 1)))
    query = pack_plan(queries, plan)
    kv = exchange(kv)
    before = lax.ppermute(kv[2:], "ctx", z_pairs(1))
    after = lax.ppermute(kv[:2], "ctx", z_pairs(-1))
    query = exchange(query)
    lists = query[:, TILE, :8].astype(jnp.int32)
    parts = []
    for first, heads in CHUNKS:
        parts.append(exchange(attend(first, heads, lists, query, kv, before, after)))
    return project(weight, parts)


def solution(mesh):
    in_specs = (
        P("dp", "ctx", None),
        P("dp", "ctx", None),
        P("dp", "ctx", None),
        P("dp", "ctx", None),
        P("dp", "ctx"),
        P("dp", None),
    )
    out_specs = P("dp", "ctx", None)
    return jax.shard_map(
        per_device, mesh=mesh, in_specs=in_specs, out_specs=out_specs, check_vma=False
    )
```

time: 307 us -> 145 us (0.47)
  the two profiles are of different devices: /device:TPU:406 before, /device:TPU:6 now
where the time goes in v1:
time: 145 us; the launch traced here: 144 us
  blocking collectives  35.1 us (24%)
  waiting for transfers between devices  33 us (23%)
  Pallas kernels  27.5 us (19%)
  starting transfers between devices  23.1 us (16%)
  between operations  14.2 us (10%)
  local copies, waits for them, and re-layouts  11 us (8%)
    all_to_all x2, blocking collectives, exchange(): return lax.all_to_all(value, 'ctx', 0, 0, axis_index_groups=groups)  35.1 us
    pallas_call x5, Pallas kernels, run(): pl.pallas_call(kernel, out_shape=outs, in_specs=specs, out_specs=jax.tree...  27.5 us
    ppermute x1, waiting for transfers between devices, per_device(): other = lax.ppermute(out_weight, ('dp', 'ctx'), mirror_pairs())  25.7 us
    ppermute x1, starting transfers between devices, per_device(): other = lax.ppermute(out_weight, ('dp', 'ctx'), mirror_pairs())  11.4 us
    unnamed x26, local copies, waits for them, and re-layouts  10.7 us
    all_to_all x2, starting transfers between devices, exchange(): return lax.all_to_all(value, 'ctx', 0, 0, axis_index_groups=groups)  9.08 us
    ppermute x1, waiting for transfers between devices, per_device(): after = lax.ppermute(kv[:2], 'ctx', z_pairs(-1))  4.19 us
  transfers between devices with their start and end apart: 7, of which 3 were waited for; matrix products, arithmetic and copies ran while one was open for 0% of the time, Pallas kernels for 15%

profile of v1, /device:TPU:6, one launch (start us, length us, event | category | flops | bytes accessed | tf_op | source)
XLA Modules:
  0.0 144.1 jit_solution(10195016002451349749)
XLA Ops:
  6.5 0.0 all-gather.3.cloned.1.call-start
  6.5 0.7 all-gather.3.cloned.1.call-update
  7.3 0.0 copy-start.3
  7.3 1.3 copy-done.3
  8.5 0.0 copy-start.4
  8.5 1.3 copy-done.4
  9.8 1.5 %pack.1 = bf16[4,2,384,384]{3,2,1,0:T(8,128)(2,1)} custom-call(bf16[1,384,1536]{2,1,0:T(8,128)(2,1)S(1)} %copy-done.3, bf16[1,384,1536]{2,1,0:T(8,128)(2,1)S(1)} %copy-done.4), custom_call_target="tpu_custom_call" | custom-call | bytes 4718592 | tf_op jit(solution)/shard_map/pack/pallas_call | solution.py:54
  11.3 0.0 copy-start.10
  11.3 0.0 copy-start.12
  11.3 4.6 %all-to-all-start.1 = ((bf16[4,2,384,384]{3,2,1,0:T(8,128)(2,1)}), bf16[4,2,384,384]{3,2,1,0:T(8,128)(2,1)S(1)}, u32[]{:S(2)}, u32[]{:S(2)}) async-start(bf16[4,2,384,384]{3,2,1,0:T(8,128)(2,1)} %pack.1), calls=%async_computation.1 | async-start | bytes 4718592 | tf_op jit(solution)/shard_map/all_to_all | solution.py:258
  15.9 0.0 all-gather.5.cloned.1.call-start
  15.9 0.0 copy-done.10
  15.9 11.4 %collective-permute-start.2 = (bf16[96,1536]{1,0:T(8,128)(2,1)S(1)}, bf16[96,1536]{1,0:T(8,128)(2,1)S(1)}, u32[]{:S(2)}, u32[]{:S(2)}) collective-permute-start(bf16[96,1536]{1,0:T(8,128)(2,1)S(1)} %copy-done.10), channel_id=1, source_target_pairs={{0,92},{1,93},{2,94},{3,95},{4,88},{5,89},{6,90},{7,91},{8,84},{9,... | collective-permute-start | bytes 884744 | tf_op jit(solution)/shard_map/ppermute | solution.py:264
  27.3 25.7 %collective-permute-done.2 = bf16[96,1536]{1,0:T(8,128)(2,1)S(1)} collective-permute-done((bf16[96,1536]{1,0:T(8,128)(2,1)S(1)}, bf16[96,1536]{1,0:T(8,128)(2,1)S(1)}, u32[]{:S(2)}, u32[]{:S(2)}) %collective-permute-start.2) | collective-permute-done | bytes 294944 | tf_op jit(solution)/shard_map/ppermute | solution.py:264
  53.0 0.0 copy-start.11
  53.0 0.7 copy-done.11
  53.7 0.0 all-gather.5.cloned.1.call-update
  54.4 0.0 copy-done.12
  54.4 0.0 copy-start.2
  54.4 0.0 all-to-all-done.1.refs_2_
  54.4 0.0 copy-start.9
  54.5 0.3 fusion.6
  54.7 1.1 copy-done.9
  55.9 1.4 collective-permute-start
  57.2 1.3 collective-permute-start.1
  58.5 0.1 fusion.5.plan
  58.6 0.0 copy-done.2
  58.6 0.3 pack_plan.1
  58.9 21.0 %all_to_all.20.refs_1_ = bf16[4,400,384]{2,1,0:T(8,128)(2,1)S(1)} all-to-all(bf16[4,400,384]{2,1,0:T(8,128)(2,1)S(1)} %pack_plan.1), channel_id=1, replica_groups={{0,1,2,3},{4,5,6,7},{8,9,10,11},{12,13,14,15},{16,17,18,19},{20,21,22,2..., dimensions={0} | all-to-all | bytes 2457600 | tf_op jit(solution)/shard_map/all_to_all | solution.py:258
  79.9 0.0 copy-start.1
  79.9 2.4 %collective-permute-done.refs_3_ = bf16[2,2,384,384]{3,2,1,0:T(8,128)(2,1)S(1)} collective-permute-done((bf16[2,2,384,384]{3,2,1,0:T(8,128)(2,1)S(1)}, bf16[2,2,384,384]{3,2,1,0:T(8,128)(2,1)S(1)}, u32[]{:S(2)}, u32[]{:S(2)}) %collective-permute-start) | collective-permute-done | bytes 1179680 | tf_op jit(solution)/shard_map/ppermute | solution.py:270
  82.4 4.2 %collective-permute-done.1.refs_4_ = bf16[2,2,384,384]{3,2,1,0:T(8,128)(2,1)S(1)} collective-permute-done((bf16[2,2,384,384]{3,2,1,0:T(8,128)(2,1)S(1)}, bf16[2,2,384,384]{3,2,1,0:T(8,128)(2,1)S(1)}, u32[]{:S(2)}, u32[]{:S(2)}) %collective-permute-start.1) | collective-permute-done | bytes 1179680 | tf_op jit(solution)/shard_map/ppermute | solution.py:271
  86.5 7.6 %attend2.1 = bf16[4,384,128]{2,1,0:T(8,128)(2,1)} custom-call(s32[4,8]{1,0:T(4,128)S(1)} %bitcast.3, bf16[4,400,384]{2,1,0:T(8,128)(2,1)S(1)} %all_to_all.20.refs_1_, bf16[4,2,384,384]{3,2,1,0:T(8,128)(2,1)} %copy-done.9, bf16[2,2,384,384]{3,2,1,0:T(8,128)(2,1)S(1)} %collective-permute-done.refs_3_, bf16[2,2,384,384]{3,2,1,0:T(8,128)(2,1)S(1)} %collective-permute-done.1.refs_4_), custom_call_target="tpu_custom_call" | custom-call | flops 5000000000 | bytes 1600000 | tf_op jit(solution)/shard_map/attend2/pallas_call | solution.py:54
  94.2 0.0 copy-done.1
  94.2 0.0 copy-start.5
  94.2 1.0 copy-done.5
  95.2 0.0 copy-start.7
  95.2 1.1 copy-done.7
  96.3 4.5 %all-to-all-start.3 = ((bf16[4,384,128]{2,1,0:T(8,128)(2,1)}), bf16[4,384,128]{2,1,0:T(8,128)(2,1)S(1)}, u32[]{:S(2)}, u32[]{:S(2)}) async-start(bf16[4,384,128]{2,1,0:T(8,128)(2,1)} %attend2.1), calls=%async_computation.3 | async-start | bytes 786432 | tf_op jit(solution)/shard_map/all_to_all | solution.py:258
  100.8 0.0 copy-start.6
  100.8 1.3 copy-done.6
  102.1 0.0 copy-start.8
  102.1 1.3 copy-done.8
  103.3 12.5 %attend0.1 = bf16[4,384,256]{2,1,0:T(8,128)(2,1)S(1)} custom-call(s32[4,8]{1,0:T(4,128)S(1)} %bitcast.4, bf16[4,400,384]{2,1,0:T(8,128)(2,1)} %copy-done.1, bf16[4,2,384,384]{3,2,1,0:T(8,128)(2,1)} %copy-done.9, bf16[2,2,384,384]{3,2,1,0:T(8,128)(2,1)S(1)} %copy-done.6, bf16[2,2,384,384]{3,2,1,0:T(8,128)(2,1)S(1)} %copy-done.8), custom_call_target="tpu_custom_call" | custom-call | flops 10000000000 | bytes 3200000 | tf_op jit(solution)/shard_map/attend0/pallas_call | solution.py:54
  115.8 0.0 all-to-all-done.3.refs_1_
  115.9 14.1 %all_to_all.21.refs_0_ = bf16[4,384,256]{2,1,0:T(8,128)(2,1)S(1)} all-to-all(bf16[4,384,256]{2,1,0:T(8,128)(2,1)S(1)} %attend0.1), channel_id=1, replica_groups={{0,1,2,3},{4,5,6,7},{8,9,10,11},{12,13,14,15},{16,17,18,19},{20,21,22,2..., dimensions={0} | all-to-all | bytes 1572864 | tf_op jit(solution)/shard_map/all_to_all | solution.py:258
  130.0 1.7 %copy-done = bf16[768,1536]{1,0:T(8,128)(2,1)S(1)} copy-done((bf16[768,1536]{1,0:T(8,128)(2,1)S(1)}, bf16[768,1536]{1,0:T(8,128)(2,1)}, u32[]{:S(2)}) %copy-start) | copy-done | bytes 2359320
  131.6 5.7 %project.1 = bf16[1,384,1536]{2,1,0:T(8,128)(2,1)} custom-call(bf16[4,384,256]{2,1,0:T(8,128)(2,1)S(1)} %all_to_all.21.refs_0_, bf16[4,384,128]{2,1,0:T(8,128)(2,1)S(1)} %all-to-all-done.3.refs_1_, bf16[768,1536]{1,0:T(8,128)(2,1)S(1)} %copy-done, bf16[768,1536]{1,0:T(8,128)(2,1)} %all-gather.5.cloned.1.call-done.refs_3_), custom_call_target="tpu_custom_call" | custom-call | flops 1811939328 | bytes 8000000 | tf_op jit(solution)/shard_map/project/pallas_call | solution.py:54
  (5 shorter events, 0.0 us)
Async XLA Ops:
  6.5 123.4 %all-gather.3.cloned.1.call-start = ((), (), s32[]{:S(2)}) async-start(), calls=%async_computation.4 | async-start | bytes 2654208 | tf_op jit(solution)/shard_map/all_gather | solution.py:261
  7.3 1.3 copy-start.3
  8.5 1.3 copy-start.4
  11.3 4.6 %copy-start.10 = (bf16[96,1536]{1,0:T(8,128)(2,1)S(1)}, bf16[96,1536]{1,0:T(8,128)(2,1)}, u32[]{:S(2)}) copy-start(bf16[96,1536]{1,0:T(8,128)(2,1)} %param.11) | copy-start | bytes 884740
  11.3 43.1 %copy-start.12 = (s32[1,1,5]{2,1,0:T(1,128)S(1)}, s32[1,1,5]{2,1,0:T(1,128)}, u32[]{:S(2)}) copy-start(s32[1,1,5]{2,1,0:T(1,128)} %param.9) | copy-start | bytes 64
  11.3 43.1 %all-to-all-start.1 = ((bf16[4,2,384,384]{3,2,1,0:T(8,128)(2,1)}), bf16[4,2,384,384]{3,2,1,0:T(8,128)(2,1)S(1)}, u32[]{:S(2)}, u32[]{:S(2)}) async-start(bf16[4,2,384,384]{3,2,1,0:T(8,128)(2,1)} %pack.1), calls=%async_computation.1 | async-start | bytes 4718592 | tf_op jit(solution)/shard_map/all_to_all | solution.py:258
  15.9 114.0 %all-gather.5.cloned.1.call-start = ((), (), s32[]{:S(2)}) async-start(), calls=%async_computation.5 | async-start | bytes 2654208 | tf_op jit(solution)/shard_map/all_gather | solution.py:261
  15.9 37.1 %collective-permute-start.2 = (bf16[96,1536]{1,0:T(8,128)(2,1)S(1)}, bf16[96,1536]{1,0:T(8,128)(2,1)S(1)}, u32[]{:S(2)}, u32[]{:S(2)}) collective-permute-start(bf16[96,1536]{1,0:T(8,128)(2,1)S(1)} %copy-done.10), channel_id=1, source_target_pairs={{0,92},{1,93},{2,94},{3,95},{4,88},{5,89},{6,90},{7,91},{8,84},{9,... | collective-permute-start | bytes 884744 | tf_op jit(solution)/shard_map/ppermute | solution.py:264
  53.0 0.7 copy-start.11
  54.4 4.2 %copy-start.2 = (bf16[1,384,1536]{2,1,0:T(8,128)(2,1)S(1)}, bf16[1,384,1536]{2,1,0:T(8,128)(2,1)}, u32[]{:S(2)}) copy-start(bf16[1,384,1536]{2,1,0:T(8,128)(2,1)} %source.1) | copy-start | bytes 3538948
  54.4 1.4 copy-start.9
  55.9 26.5 %collective-permute-start = (bf16[2,2,384,384]{3,2,1,0:T(8,128)(2,1)S(1)}, bf16[2,2,384,384]{3,2,1,0:T(8,128)(2,1)S(1)}, u32[]{:S(2)}, u32[]{:S(2)}) collective-permute-start(bf16[2,2,384,384]{3,2,1,0:T(8,128)(2,1)S(1)} %get-tuple-element.6), channel_id=1, source_target_pairs={{0,4},{1,5},{2,6},{3,7},{4,8},{5,9},{6,10},{7,11},{8,12},{9,13},{1... | collective-permute-start | bytes 3538952 | tf_op jit(solution)/shard_map/ppermute | solution.py:270
  57.2 29.3 %collective-permute-start.1 = (bf16[2,2,384,384]{3,2,1,0:T(8,128)(2,1)S(1)}, bf16[2,2,384,384]{3,2,1,0:T(8,128)(2,1)S(1)}, u32[]{:S(2)}, u32[]{:S(2)}) collective-permute-start(bf16[2,2,384,384]{3,2,1,0:T(8,128)(2,1)S(1)} %get-tuple-element.5), channel_id=1, source_target_pairs={{4,0},{5,1},{6,2},{7,3},{8,4},{9,5},{10,6},{11,7},{12,8},{13,9},{1... | collective-permute-start | bytes 3538952 | tf_op jit(solution)/shard_map/ppermute | solution.py:271
  79.9 14.3 %copy-start.1 = (bf16[4,400,384]{2,1,0:T(8,128)(2,1)}, bf16[4,400,384]{2,1,0:T(8,128)(2,1)S(1)}, u32[]{:S(2)}) copy-start(bf16[4,400,384]{2,1,0:T(8,128)(2,1)S(1)} %all_to_all.20.refs_1_) | copy-start | bytes 3686404
  94.2 1.0 copy-start.5
  95.2 1.1 copy-start.7
  96.3 19.5 %all-to-all-start.3 = ((bf16[4,384,128]{2,1,0:T(8,128)(2,1)}), bf16[4,384,128]{2,1,0:T(8,128)(2,1)S(1)}, u32[]{:S(2)}, u32[]{:S(2)}) async-start(bf16[4,384,128]{2,1,0:T(8,128)(2,1)} %attend2.1), calls=%async_computation.3 | async-start | bytes 786432 | tf_op jit(solution)/shard_map/all_to_all | solution.py:258
  100.8 1.3 copy-start.6
  102.1 1.3 copy-start.8
  130.0 1.7 %copy-start = (bf16[768,1536]{1,0:T(8,128)(2,1)S(1)}, bf16[768,1536]{1,0:T(8,128)(2,1)}, u32[]{:S(2)}) copy-start(bf16[768,1536]{1,0:T(8,128)(2,1)} %all-gather.3.cloned.1.call-done.refs_2_) | copy-start | bytes 7077892
Sparse Core Ops, SparseCore 0:
  9.5 36.5 all-gather.2
  53.9 30.0 all-gather.4

commit v2 on v1

v2 whole, which is shorter than its diff:
```python
import math

import jax
import jax.numpy as jnp
from jax import lax
from jax.experimental import pallas as pl
from jax.experimental.pallas import tpu as pltpu
from jax.sharding import PartitionSpec as P

HD = 128
SLOTS = 5
TILE = 384
DOUT = 1536
RING = 4
RUNS = 8
HEADS_HERE = 3
GC = HEADS_HERE * HD
EXTRA = 16
CHUNKS = ((0, 2), (2, 1))
FACTOR = math.log2(math.e) / math.sqrt(HD)
VMEM = 62 * 1024 * 1024


def z_pairs(by):
    return [
        (z * RING + y, (z + by) * RING + y)
        for z in range(RUNS)
        for y in range(RING)
        if 0 <= z + by < RUNS
    ]


def mirror_pairs():
    pairs = []
    for x in range(4):
        for high in range(2):
            for core in range(2):
                for z in range(RUNS):
                    for y in range(RING):
                        here = (x * 4 + high * 2 + core) * 32 + z * RING + y
                        there = (x * 4 + (1 - high) * 2 + core) * 32 + (RUNS - 1 - z) * RING + y
                        pairs.append((here, there))
    return pairs


def call(kernel, name, outs, scratch, flops, nbytes, smem):
    any_spec = pl.BlockSpec(memory_space=pl.ANY)

    def run(*args):
        specs = [
            pl.BlockSpec(memory_space=pltpu.SMEM) if i < smem else any_spec
            for i in range(len(args))
        ]
        return pl.pallas_call(
            kernel,
            out_shape=outs,
            in_specs=specs,
            out_specs=jax.tree.map(lambda _: any_spec, outs),
            scratch_shapes=scratch,
            compiler_params=pltpu.CompilerParams(vmem_limit_bytes=VMEM),
            cost_estimate=pl.CostEstimate(flops=flops, bytes_accessed=nbytes, transcendentals=0),
            name=name,
        )(*args)

    return run


def pack(arrays, plan=None):
    tall = TILE * len(arrays) + (0 if plan is None else EXTRA)
    count = len(arrays)

    def kernel(*refs):
        sources, (out, block, in_sems, out_sems) = refs[:count], refs[-4:]
        loads, stores = [], []
        for i, source in enumerate(sources):
            for at in range(RING):
                n = len(loads)
                loads.append(
                    pltpu.make_async_copy(
                        source.at[0, :, pl.ds(at * GC, GC)], block.at[n], in_sems.at[n]
                    )
                )
                stores.append(
                    pltpu.make_async_copy(
                        block.at[n], out.at[at, pl.ds(i * TILE, TILE)], out_sems.at[n]
                    )
                )
                loads[-1].start()
        if plan is not None:
            for at in range(RING):
                stores.append(
                    pltpu.make_async_copy(
                        refs[count],
                        out.at[at, pl.ds(count * TILE, EXTRA)],
                        out_sems.at[len(stores)],
                    )
                )
                stores[-1].start()
        for load, store in zip(loads, stores):
            load.wait()
            store.start()
        for store in stores:
            store.wait()

    return call(
        kernel,
        f"pack{count}",
        jax.ShapeDtypeStruct((RING, tall, GC), jnp.bfloat16),
        [
            pltpu.VMEM((RING * count, TILE, GC), jnp.bfloat16),
            pltpu.SemaphoreType.DMA((RING * count,)),
            pltpu.SemaphoreType.DMA((RING * (count + 1),)),
        ],
        0,
        RING * tall * GC * 4,
        0,
    )(*arrays, *([] if plan is None else [plan]))


def attend_kernel(first, heads, lists, *refs):
    kv_in, q_in, before, after, out, qb, kvb, ob, in_sems, out_sems = refs
    columns = pl.ds(first * HD, heads * HD)
    base = lax.div(lax.axis_index("ctx"), RING) * RING
    copies = []
    for source, target in (
        (q_in.at[:, pl.ds(0, TILE), columns], qb),
        (kv_in.at[:, :, columns], kvb.at[pl.ds(0, 4)]),
        (before.at[:, :, columns], kvb.at[pl.ds(4, 2)]),
        (after.at[:, :, columns], kvb.at[pl.ds(6, 2)]),
    ):
        copies.append(pltpu.make_async_copy(source, target, in_sems.at[len(copies)]))
        copies[-1].start()
    for copy in copies:
        copy.wait()
    half = TILE // 2

    def tile_of(at, count):
        slots = []
        for s in range(count):
            tile = lists[at, s] - base
            slots.append(tile + jnp.where(tile < 0, 6, jnp.where(tile < RING, 0, 2)))

        def column_of(part, col):
            return jnp.concatenate(
                [kvb[slot, pl.ds(part * TILE, TILE), col] for slot in slots], axis=0
            )

        def score(rows, col):
            scores = lax.dot_general(
                qb[at, rows, col],
                column_of(0, col),
                (((1,), (1,)), ((), ())),
                preferred_element_type=jnp.float32,
            )
            return scores, jnp.max(scores, axis=1, keepdims=True)

        def mix(rows, col, scores, peak):
            probs = jnp.exp2((scores - peak) * FACTOR).astype(jnp.bfloat16)
            ones = jnp.ones((count * TILE, HD), jnp.bfloat16)
            value = jnp.concatenate([column_of(1, col), ones], axis=1)
            total = jnp.dot(probs, value, preferred_element_type=jnp.float32)
            ob[at, rows, col] = (total[:, :HD] / total[:, HD:]).astype(jnp.bfloat16)

        for head in range(heads):
            col = pl.ds(head * HD, HD)
            upper, lower = pl.ds(0, half), pl.ds(half, half)
            first_scores = score(upper, col)
            second_scores = score(lower, col)
            mix(upper, col, *first_scores)
            mix(lower, col, *second_scores)

    def body(at, carry):
        live = lists[at, SLOTS]
        for count in range(1, SLOTS + 1):

            @pl.when(live == count)
            def _():
                tile_of(at, count)

        return carry

    lax.fori_loop(0, RING, body, 0)
    last = pltpu.make_async_copy(ob, out, out_sems.at[0])
    last.start()
    last.wait()


def attend(first, heads, lists, *arrays):
    wide = heads * HD
    return call(
        lambda *refs: attend_kernel(first, heads, *refs),
        f"attend{first}",
        jax.ShapeDtypeStruct((RING, TILE, wide), jnp.bfloat16),
        [
            pltpu.VMEM((RING, TILE, wide), jnp.bfloat16),
            pltpu.VMEM((2 * RING, 2 * TILE, wide), jnp.bfloat16),
            pltpu.VMEM((RING, TILE, wide), jnp.bfloat16),
            pltpu.SemaphoreType.DMA((4,)),
            pltpu.SemaphoreType.DMA((1,)),
        ],
        heads * 5_000_000_000,
        heads * 1_600_000,
        1,
    )(lists, *arrays)


def project(first, heads, part, near, far, total=None):
    wide = heads * HD
    deep = RING * wide
    pieces = []
    for shard in range(4):
        low, high = max(shard * 96, first * HD), min(shard * 96 + 96, first * HD + wide)
        if low < high:
            pieces.append((low - first * HD, high - low, shard % 2, shard // 2, low - shard * 96))

    def kernel(*refs):
        part_in, near_in, far_in, *others = refs
        if total is None:
            out, rows, weights, result, sems = others
        else:
            total_in, out, rows, weights, result, sums, sems = others
        z_half = lax.rem(lax.div(lax.axis_index("dp"), 2), 2)

        def weight_copies(own):
            copies = []
            for g in range(RING):
                for to, count, core, half, at in pieces:
                    source = near_in if half == own else far_in
                    copies.append(
                        pltpu.make_async_copy(
                            source.at[pl.ds((2 * g + core) * 96 + at, count)],
                            weights.at[pl.ds(g * wide + to, count)],
                            sems.at[len(copies)],
                        )
                    )
            return copies

        for own in range(2):

            @pl.when(z_half == own)
            def _():
                for copy in weight_copies(own):
                    copy.start()

        waits = weight_copies(0)
        for g in range(RING):
            copy = pltpu.make_async_copy(
                part_in.at[g], rows.at[:, pl.ds(g * wide, wide)], sems.at[len(waits)]
            )
            copy.start()
            waits.append(copy)
        if total is not None:
            copy = pltpu.make_async_copy(total_in, sums, sems.at[len(waits)])
            copy.start()
            waits.append(copy)
        for copy in waits:
            copy.wait()
        stores = []
        for step in range(DOUT // 512):
            col = pl.ds(step * 512, 512)
            product = jnp.dot(rows[...], weights[:, col], preferred_element_type=jnp.float32)
            if total is not None:
                product = (product + sums[:, col]).astype(jnp.bfloat16)
            result[:, col] = product
            target = out.at[:, col] if total is None else out.at[0, :, col]
            stores.append(pltpu.make_async_copy(result.at[:, col], target, sems.at[step]))
            stores[-1].start()
        for store in stores:
            store.wait()

    kind = jnp.float32 if total is None else jnp.bfloat16
    shape = (TILE, DOUT) if total is None else (1, TILE, DOUT)
    scratch = [
        pltpu.VMEM((TILE, deep), jnp.bfloat16),
        pltpu.VMEM((deep, DOUT), jnp.bfloat16),
        pltpu.VMEM((TILE, DOUT), kind),
    ]
    if total is not None:
        scratch.append(pltpu.VMEM((TILE, DOUT), jnp.float32))
    scratch.append(pltpu.SemaphoreType.DMA((RING * len(pieces) + RING + 1,)))
    return call(
        kernel,
        f"project{first}",
        jax.ShapeDtypeStruct(shape, kind),
        scratch,
        2 * TILE * deep * DOUT,
        8_000_000,
        0,
    )(part, near, far, *([] if total is None else [total]))


def per_device(queries, key_rows, value_rows, tile_lists, tile_counts, out_weight):
    groups = [[z * RING + y for y in range(RING)] for z in range(RUNS)]
    pairs = [[x * 4 + high * 2 + core for x in range(4) for core in range(2)] for high in range(2)]

    def exchange(value):
        return lax.all_to_all(value, "ctx", 0, 0, axis_index_groups=groups)

    def gather(value):
        return lax.all_gather(value, "dp", axis=0, tiled=True, axis_index_groups=pairs)

    def halo(value):
        return (
            lax.ppermute(value[2:], "ctx", z_pairs(1)),
            lax.ppermute(value[:2], "ctx", z_pairs(-1)),
        )

    def after(values, done):
        return lax.optimization_barrier((values, done))[0]

    packed = pack((key_rows, value_rows))
    out_weight, queries, tile_lists, tile_counts = after(
        (out_weight, queries, tile_lists, tile_counts), packed
    )
    plan = jnp.concatenate([tile_lists[0], tile_counts], axis=1).astype(jnp.bfloat16)
    plan = jnp.pad(plan, ((0, EXTRA - 1), (0, GC - SLOTS - 1)))
    near = gather(out_weight)
    other = lax.ppermute(out_weight, ("dp", "ctx"), mirror_pairs())
    key_values = exchange(packed)
    packed, key_values, other = lax.optimization_barrier(
        (pack((queries,), plan), key_values, other)
    )
    far = gather(other)
    query = exchange(packed)
    edges = halo(key_values)
    lists = query[:, TILE, :8].astype(jnp.int32)
    query, edges = lax.optimization_barrier((query, edges))
    parts = []
    for first, heads in CHUNKS:
        mixed = attend(first, heads, lists, key_values, query, *edges)
        if parts:
            mixed, parts[-1] = lax.optimization_barrier((mixed, parts[-1]))
        else:
            mixed, query = lax.optimization_barrier((mixed, query))
        parts.append(exchange(mixed))
    total = project(*CHUNKS[0], parts[0], near, far)
    return project(*CHUNKS[1], parts[1], near, far, total)


def solution(mesh):
    in_specs = (
        P("dp", "ctx", None),
        P("dp", "ctx", None),
        P("dp", "ctx", None),
        P("dp", "ctx", None),
        P("dp", "ctx"),
        P("dp", None),
    )
    out_specs = P("dp", "ctx", None)
    return jax.shard_map(
        per_device, mesh=mesh, in_specs=in_specs, out_specs=out_specs, check_vma=False
    )
```

time: 145 us -> 135 us (0.931)
  blocking collectives: 35.1 us -> 21 us
  local copies, waits for them, and re-layouts: 11 us -> 4.56 us
  starting transfers between devices: 23.1 us -> 26.6 us
  Pallas kernels: 27.5 us -> 30.4 us
  waiting for transfers between devices: 33 us -> 34.9 us
    all_to_all x2 -> x1, blocking collectives: 35.1 us -> 21 us  [exchange(): return lax.all_to_all(value, 'ctx', 0, 0, axis_index_groups=groups)]
    unnamed x26 -> x18, local copies, waits for them, and re-layouts: 10.7 us -> 2.6 us
    all_to_all x2 -> x3, waiting for transfers between devices: 0.01 us -> 6.58 us  [exchange(): return lax.all_to_all(value, 'ctx', 0, 0, axis_index_groups=groups)]
    ppermute x1, waiting for transfers between devices: 25.7 us -> 21.9 us  [per_device(): other = lax.ppermute(out_weight, ('dp', 'ctx'), mirror_pairs())]
    all_to_all x2 -> x3, starting transfers between devices: 9.08 us -> 12.5 us  [exchange(): return lax.all_to_all(value, 'ctx', 0, 0, axis_index_groups=groups)]
    pallas_call x5 -> x6, Pallas kernels: 27.5 us -> 30.4 us  [run(): pl.pallas_call(kernel, out_shape=outs, in_specs=specs, out_specs=jax.tree...]
    slice x1, local copies, waits for them, and re-layouts: 0.26 us -> 1.96 us  [halo(): value[:2]]
  transfers between devices with their start and end apart: 7 -> 8, of which waited for: 3 -> 5; matrix products, arithmetic and copies ran while one was open for 0% -> 2% of each run, Pallas kernels for 15% -> 18%
where the time goes in v2:
time: 135 us; the launch traced here: 133 us
  waiting for transfers between devices  34.9 us (26%)
  Pallas kernels  30.4 us (23%)
  starting transfers between devices  26.6 us (20%)
  blocking collectives  21 us (16%)
  between operations  14.2 us (11%)
  local copies, waits for them, and re-layouts  4.56 us (3%)
    pallas_call x6, Pallas kernels, run(): pl.pallas_call(kernel, out_shape=outs, in_specs=specs, out_specs=jax.tree...  30.4 us
    ppermute x1, waiting for transfers between devices, per_device(): other = lax.ppermute(out_weight, ('dp', 'ctx'), mirror_pairs())  21.9 us
    all_to_all x1, blocking collectives, exchange(): return lax.all_to_all(value, 'ctx', 0, 0, axis_index_groups=groups)  21 us
    all_to_all x3, starting transfers between devices, exchange(): return lax.all_to_all(value, 'ctx', 0, 0, axis_index_groups=groups)  12.5 us
    ppermute x1, starting transfers between devices, per_device(): other = lax.ppermute(out_weight, ('dp', 'ctx'), mirror_pairs())  11.4 us
    all_to_all x3, waiting for transfers between devices, exchange(): return lax.all_to_all(value, 'ctx', 0, 0, axis_index_groups=groups)  6.58 us
    ppermute x1, waiting for transfers between devices, halo(): lax.ppermute(value[:2], 'ctx', z_pairs(-1))  4.19 us
  transfers between devices with their start and end apart: 8, of which 5 were waited for; matrix products, arithmetic and copies ran while one was open for 2% of the time, Pallas kernels for 18%

profile of v2, /device:TPU:6, one launch (start us, length us, event | category | flops | bytes accessed | tf_op | source)
XLA Modules:
  0.0 133.1 jit_solution(4307674143573710550)
XLA Ops:
  6.5 0.0 all-gather.3.cloned.1.call-start
  6.5 2.6 %pack2.1 = bf16[4,768,384]{2,1,0:T(8,128)(2,1)} custom-call(bf16[1,384,1536]{2,1,0:T(8,128)(2,1)} %refs_0_.1, bf16[1,384,1536]{2,1,0:T(8,128)(2,1)} %refs_1_.1), custom_call_target="tpu_custom_call" | custom-call | bytes 4718592 | tf_op jit(solution)/shard_map/pack2/pallas_call | solution.py:54
  9.1 0.0 all-gather.3.cloned.1.call-update
  9.2 0.0 copy-start.4
  9.2 0.0 copy-start.8
  9.2 4.6 %all-to-all-start = ((bf16[4,768,384]{2,1,0:T(8,128)(2,1)}), bf16[4,768,384]{2,1,0:T(8,128)(2,1)}, u32[]{:S(2)}, u32[]{:S(2)}) async-start(bf16[4,768,384]{2,1,0:T(8,128)(2,1)} %pack2.1), calls=%async_computation | async-start | bytes 4718592 | tf_op jit(solution)/shard_map/all_to_all | solution.py:297
  13.8 0.0 all-gather.5.cloned.1.call-start
  13.9 0.0 copy-done.4
  13.9 11.4 %collective-permute-start = (bf16[96,1536]{1,0:T(8,128)(2,1)S(1)}, bf16[96,1536]{1,0:T(8,128)(2,1)S(1)}, u32[]{:S(2)}, u32[]{:S(2)}) collective-permute-start(bf16[96,1536]{1,0:T(8,128)(2,1)S(1)} %copy-done.4), channel_id=1, source_target_pairs={{0,92},{1,93},{2,94},{3,95},{4,88},{5,89},{6,90},{7,91},{8,84},{9,... | collective-permute-start | bytes 884744 | tf_op jit(solution)/shard_map/ppermute | solution.py:318
  26.0 0.0 copy-done.8
  26.0 0.7 fusion.5.refs_1_
  26.7 2.7 %pack1.1 = bf16[4,400,384]{2,1,0:T(8,128)(2,1)} custom-call(bf16[1,384,1536]{2,1,0:T(8,128)(2,1)} %refs_0_.2, bf16[16,384]{1,0:T(8,128)(2,1)} %fusion.5.refs_1_), custom_call_target="tpu_custom_call" | custom-call | bytes 2457600 | tf_op jit(solution)/shard_map/pack1/pallas_call | solution.py:54
  29.4 21.9 %collective-permute-done = bf16[96,1536]{1,0:T(8,128)(2,1)S(1)} collective-permute-done((bf16[96,1536]{1,0:T(8,128)(2,1)S(1)}, bf16[96,1536]{1,0:T(8,128)(2,1)S(1)}, u32[]{:S(2)}, u32[]{:S(2)}) %collective-permute-start) | collective-permute-done | bytes 294944 | tf_op jit(solution)/shard_map/ppermute | solution.py:318
  51.3 0.0 copy-start.5
  51.3 0.0 all-to-all-done.refs_1_
  51.3 0.7 copy-done.5
  52.0 0.0 all-gather.5.cloned.1.call-update
  52.0 0.0 copy-start
  52.0 2.0 %fusion.6 = (bf16[2,768,384]{2,1,0:T(8,128)(2,1)S(1)}, bf16[2,768,384]{2,1,0:T(8,128)(2,1)S(1)}) fusion(bf16[4,768,384]{2,1,0:T(8,128)(2,1)} %all-to-all-done.refs_1_), kind=kLoop, calls=%fused_computation.10 | loop fusion | bytes 4718592 | tf_op jit(solution)/shard_map/slice | solution.py:305
  54.0 1.4 %collective-permute-start.1 = (bf16[2,768,384]{2,1,0:T(8,128)(2,1)S(1)}, bf16[2,768,384]{2,1,0:T(8,128)(2,1)S(1)}, u32[]{:S(2)}, u32[]{:S(2)}) collective-permute-start(bf16[2,768,384]{2,1,0:T(8,128)(2,1)S(1)} %get-tuple-element.34), channel_id=1, source_target_pairs={{0,4},{1,5},{2,6},{3,7},{4,8},{5,9},{6,10},{7,11},{8,12},{9,13},{1... | collective-permute-start | bytes 3538952 | tf_op jit(solution)/shard_map/ppermute | solution.py:304
  55.4 1.3 collective-permute-start.2
  56.7 0.0 copy-done
  56.7 21.0 %all_to_all.20.refs_2_ = bf16[4,400,384]{2,1,0:T(8,128)(2,1)S(1)} all-to-all(bf16[4,400,384]{2,1,0:T(8,128)(2,1)S(1)} %copy-done), channel_id=1, replica_groups={{0,1,2,3},{4,5,6,7},{8,9,10,11},{12,13,14,15},{16,17,18,19},{20,21,22,2..., dimensions={0} | all-to-all | bytes 2457600 | tf_op jit(solution)/shard_map/all_to_all | solution.py:297
  77.7 0.0 copy-start.3
  77.7 0.6 slice_convert_fusion
  78.3 2.2 %collective-permute-done.1.refs_3_ = bf16[2,768,384]{2,1,0:T(8,128)(2,1)S(1)} collective-permute-done((bf16[2,768,384]{2,1,0:T(8,128)(2,1)S(1)}, bf16[2,768,384]{2,1,0:T(8,128)(2,1)S(1)}, u32[]{:S(2)}, u32[]{:S(2)}) %collective-permute-start.1) | collective-permute-done | bytes 1179680 | tf_op jit(solution)/shard_map/ppermute | solution.py:304
  80.5 0.0 copy-start.6
  80.5 4.2 %collective-permute-done.2.refs_4_ = bf16[2,768,384]{2,1,0:T(8,128)(2,1)S(1)} collective-permute-done((bf16[2,768,384]{2,1,0:T(8,128)(2,1)S(1)}, bf16[2,768,384]{2,1,0:T(8,128)(2,1)S(1)}, u32[]{:S(2)}, u32[]{:S(2)}) %collective-permute-start.2) | collective-permute-done | bytes 1179680 | tf_op jit(solution)/shard_map/ppermute | solution.py:305
  84.7 0.0 copy-done.6
  84.7 0.0 copy-start.7
  84.7 1.1 copy-done.7
  85.8 0.0 copy-done.3
  85.8 10.0 %attend0.1 = bf16[4,384,256]{2,1,0:T(8,128)(2,1)} custom-call(s32[4,8]{1,0:T(4,128)} %bitcast.3, bf16[4,768,384]{2,1,0:T(8,128)(2,1)} %all-to-all-done.refs_1_, bf16[4,400,384]{2,1,0:T(8,128)(2,1)} %copy-done.3, bf16[2,768,384]{2,1,0:T(8,128)(2,1)} %copy-done.6, bf16[2,768,384]{2,1,0:T(8,128)(2,1)} %copy-done.7), custom_call_target="tpu_custom_call" | custom-call | flops 10000000000 | bytes 3200000 | tf_op jit(solution)/shard_map/attend0/pallas_call | solution.py:54
  95.9 4.4 %all-to-all-start.2 = ((bf16[4,384,256]{2,1,0:T(8,128)(2,1)}), bf16[4,384,256]{2,1,0:T(8,128)(2,1)S(1)}, u32[]{:S(2)}, u32[]{:S(2)}) async-start(bf16[4,384,256]{2,1,0:T(8,128)(2,1)} %attend0.1), calls=%async_computation.2 | async-start | bytes 1572864 | tf_op jit(solution)/shard_map/all_to_all | solution.py:297
  100.3 6.5 %attend2.1 = bf16[4,384,128]{2,1,0:T(8,128)(2,1)} custom-call(s32[4,8]{1,0:T(4,128)} %bitcast.4, bf16[4,768,384]{2,1,0:T(8,128)(2,1)} %all-to-all-done.refs_1_, bf16[4,400,384]{2,1,0:T(8,128)(2,1)} %copy-done.3, bf16[2,768,384]{2,1,0:T(8,128)(2,1)} %copy-done.6, bf16[2,768,384]{2,1,0:T(8,128)(2,1)} %copy-done.7), custom_call_target="tpu_custom_call" | custom-call | flops 5000000000 | bytes 1600000 | tf_op jit(solution)/shard_map/attend2/pallas_call | solution.py:54
  106.9 3.8 %all-to-all-done.2.refs_0_ = bf16[4,384,256]{2,1,0:T(8,128)(2,1)S(1)} async-done(((bf16[4,384,256]{2,1,0:T(8,128)(2,1)}), bf16[4,384,256]{2,1,0:T(8,128)(2,1)S(1)}, u32[]{:S(2)}, u32[]{:S(2)}) %all-to-all-start.2) | async-done | bytes 786464 | tf_op jit(solution)/shard_map/all_to_all | solution.py:297
  110.7 0.0 copy-start.1
  110.7 3.5 %all-to-all-start.3 = ((bf16[4,384,128]{2,1,0:T(8,128)(2,1)}), bf16[4,384,128]{2,1,0:T(8,128)(2,1)S(1)}, u32[]{:S(2)}, u32[]{:S(2)}) async-start(bf16[4,384,128]{2,1,0:T(8,128)(2,1)} %attend2.1), calls=%async_computation.3 | async-start | bytes 786432 | tf_op jit(solution)/shard_map/all_to_all | solution.py:297
  114.2 0.0 all-gather.3.cloned.1.call-done.refs_1_
  114.2 0.0 all-gather.5.cloned.1.call-done.refs_2_
  114.2 0.0 copy-done.1
  114.3 4.5 %project0.1.refs_3_ = f32[384,1536]{1,0:T(8,128)} custom-call(bf16[4,384,256]{2,1,0:T(8,128)(2,1)} %copy-done.1, bf16[768,1536]{1,0:T(8,128)(2,1)} %all-gather.3.cloned.1.call-done.refs_1_, bf16[768,1536]{1,0:T(8,128)(2,1)} %all-gather.5.cloned.1.call-done.refs_2_), custom_call_target="tpu_custom_call" | custom-call | flops 1207959552 | bytes 8000000 | tf_op jit(solution)/shard_map/project0/pallas_call | solution.py:54
  118.8 2.7 %all-to-all-done.3.refs_0_ = bf16[4,384,128]{2,1,0:T(8,128)(2,1)S(1)} async-done(((bf16[4,384,128]{2,1,0:T(8,128)(2,1)}), bf16[4,384,128]{2,1,0:T(8,128)(2,1)S(1)}, u32[]{:S(2)}, u32[]{:S(2)}) %all-to-all-start.3) | async-done | bytes 393248 | tf_op jit(solution)/shard_map/all_to_all | solution.py:297
  121.5 0.0 copy-start.2
  121.5 0.7 copy-done.2
  122.3 3.9 %project2.1 = bf16[1,384,1536]{2,1,0:T(8,128)(2,1)} custom-call(bf16[4,384,128]{2,1,0:T(8,128)(2,1)} %copy-done.2, bf16[768,1536]{1,0:T(8,128)(2,1)} %all-gather.3.cloned.1.call-done.refs_1_, bf16[768,1536]{1,0:T(8,128)(2,1)} %all-gather.5.cloned.1.call-done.refs_2_, f32[384,1536]{1,0:T(8,128)} %project0.1.refs_3_), custom_call_target="tpu_custom_call" | custom-call | flops 603979776 | bytes 8000000 | tf_op jit(solution)/shard_map/project2/pallas_call | solution.py:54
  (1 shorter events, 0.0 us)
Async XLA Ops:
  6.5 107.7 %all-gather.3.cloned.1.call-start = ((), (), s32[]{:S(2)}) async-start(), calls=%async_computation.4 | async-start | bytes 2654208 | tf_op jit(solution)/shard_map/all_gather | solution.py:300
  9.2 4.7 %copy-start.4 = (bf16[96,1536]{1,0:T(8,128)(2,1)S(1)}, bf16[96,1536]{1,0:T(8,128)(2,1)}, u32[]{:S(2)}) copy-start(bf16[96,1536]{1,0:T(8,128)(2,1)} %param.11) | copy-start | bytes 884740
  9.2 16.8 %copy-start.8 = (s32[1,1,5]{2,1,0:T(1,128)S(1)}, s32[1,1,5]{2,1,0:T(1,128)}, u32[]{:S(2)}) copy-start(s32[1,1,5]{2,1,0:T(1,128)} %param.9) | copy-start | bytes 64
  9.2 42.1 %all-to-all-start = ((bf16[4,768,384]{2,1,0:T(8,128)(2,1)}), bf16[4,768,384]{2,1,0:T(8,128)(2,1)}, u32[]{:S(2)}, u32[]{:S(2)}) async-start(bf16[4,768,384]{2,1,0:T(8,128)(2,1)} %pack2.1), calls=%async_computation | async-start | bytes 4718592 | tf_op jit(solution)/shard_map/all_to_all | solution.py:297
  13.8 100.4 %all-gather.5.cloned.1.call-start = ((), (), s32[]{:S(2)}) async-start(), calls=%async_computation.5 | async-start | bytes 2654208 | tf_op jit(solution)/shard_map/all_gather | solution.py:300
  13.9 37.4 %collective-permute-start = (bf16[96,1536]{1,0:T(8,128)(2,1)S(1)}, bf16[96,1536]{1,0:T(8,128)(2,1)S(1)}, u32[]{:S(2)}, u32[]{:S(2)}) collective-permute-start(bf16[96,1536]{1,0:T(8,128)(2,1)S(1)} %copy-done.4), channel_id=1, source_target_pairs={{0,92},{1,93},{2,94},{3,95},{4,88},{5,89},{6,90},{7,91},{8,84},{9,... | collective-permute-start | bytes 884744 | tf_op jit(solution)/shard_map/ppermute | solution.py:318
  51.3 0.7 copy-start.5
  52.0 4.6 %copy-start = (bf16[4,400,384]{2,1,0:T(8,128)(2,1)S(1)}, bf16[4,400,384]{2,1,0:T(8,128)(2,1)}, u32[]{:S(2)}) copy-start(bf16[4,400,384]{2,1,0:T(8,128)(2,1)} %pack1.1) | copy-start | bytes 3686404
  54.0 26.5 %collective-permute-start.1 = (bf16[2,768,384]{2,1,0:T(8,128)(2,1)S(1)}, bf16[2,768,384]{2,1,0:T(8,128)(2,1)S(1)}, u32[]{:S(2)}, u32[]{:S(2)}) collective-permute-start(bf16[2,768,384]{2,1,0:T(8,128)(2,1)S(1)} %get-tuple-element.34), channel_id=1, source_target_pairs={{0,4},{1,5},{2,6},{3,7},{4,8},{5,9},{6,10},{7,11},{8,12},{9,13},{1... | collective-permute-start | bytes 3538952 | tf_op jit(solution)/shard_map/ppermute | solution.py:304
  55.4 29.4 %collective-permute-start.2 = (bf16[2,768,384]{2,1,0:T(8,128)(2,1)S(1)}, bf16[2,768,384]{2,1,0:T(8,128)(2,1)S(1)}, u32[]{:S(2)}, u32[]{:S(2)}) collective-permute-start(bf16[2,768,384]{2,1,0:T(8,128)(2,1)S(1)} %get-tuple-element.33), channel_id=1, source_target_pairs={{4,0},{5,1},{6,2},{7,3},{8,4},{9,5},{10,6},{11,7},{12,8},{13,9},{1... | collective-permute-start | bytes 3538952 | tf_op jit(solution)/shard_map/ppermute | solution.py:305
  77.7 8.2 %copy-start.3 = (bf16[4,400,384]{2,1,0:T(8,128)(2,1)}, bf16[4,400,384]{2,1,0:T(8,128)(2,1)S(1)}, u32[]{:S(2)}) copy-start(bf16[4,400,384]{2,1,0:T(8,128)(2,1)S(1)} %all_to_all.20.refs_2_) | copy-start | bytes 3686404
  80.5 4.2 %copy-start.6 = (bf16[2,768,384]{2,1,0:T(8,128)(2,1)}, bf16[2,768,384]{2,1,0:T(8,128)(2,1)S(1)}, u32[]{:S(2)}) copy-start(bf16[2,768,384]{2,1,0:T(8,128)(2,1)S(1)} %collective-permute-done.1.refs_3_) | copy-start | bytes 3538948
  84.7 1.1 copy-start.7
  95.9 14.8 %all-to-all-start.2 = ((bf16[4,384,256]{2,1,0:T(8,128)(2,1)}), bf16[4,384,256]{2,1,0:T(8,128)(2,1)S(1)}, u32[]{:S(2)}, u32[]{:S(2)}) async-start(bf16[4,384,256]{2,1,0:T(8,128)(2,1)} %attend0.1), calls=%async_computation.2 | async-start | bytes 1572864 | tf_op jit(solution)/shard_map/all_to_all | solution.py:297
  110.7 3.5 %copy-start.1 = (bf16[4,384,256]{2,1,0:T(8,128)(2,1)}, bf16[4,384,256]{2,1,0:T(8,128)(2,1)S(1)}, u32[]{:S(2)}) copy-start(bf16[4,384,256]{2,1,0:T(8,128)(2,1)S(1)} %all-to-all-done.2.refs_0_) | copy-start | bytes 2359300
  110.7 10.8 %all-to-all-start.3 = ((bf16[4,384,128]{2,1,0:T(8,128)(2,1)}), bf16[4,384,128]{2,1,0:T(8,128)(2,1)S(1)}, u32[]{:S(2)}, u32[]{:S(2)}) async-start(bf16[4,384,128]{2,1,0:T(8,128)(2,1)} %attend2.1), calls=%async_computation.3 | async-start | bytes 786432 | tf_op jit(solution)/shard_map/all_to_all | solution.py:297
  121.5 0.7 copy-start.2
Sparse Core Ops, SparseCore 0:
  9.5 36.6 all-gather.2
  52.1 29.9 all-gather.4

commit v3 on v2

--- a/solution.py
+++ b/solution.py
@@ -16,7 +16,7 @@
 HEADS_HERE = 3
 GC = HEADS_HERE * HD
 EXTRA = 16
-CHUNKS = ((0, 2), (2, 1))
+CHUNKS = ((0, HEADS_HERE),)
 FACTOR = math.log2(math.e) / math.sqrt(HD)
 VMEM = 62 * 1024 * 1024
 
@@ -204,7 +204,7 @@
     )(lists, *arrays)
 
 
-def project(first, heads, part, near, far, total=None):
+def project(first, heads, part, near, far):
     wide = heads * HD
     deep = RING * wide
     pieces = []
@@ -215,10 +215,7 @@
 
     def kernel(*refs):
         part_in, near_in, far_in, *others = refs
-        if total is None:
-            out, rows, weights, result, sems = others
-        else:
-            total_in, out, rows, weights, result, sums, sems = others
+        out, rows, weights, result, sems = others
         z_half = lax.rem(lax.div(lax.axis_index("dp"), 2), 2)
 
         def weight_copies(own):
@@ -249,44 +246,35 @@
             )
             copy.start()
             waits.append(copy)
-        if total is not None:
-            copy = pltpu.make_async_copy(total_in, sums, sems.at[len(waits)])
-            copy.start()
-            waits.append(copy)
         for copy in waits:
             copy.wait()
         stores = []
         for step in range(DOUT // 512):
             col = pl.ds(step * 512, 512)
             product = jnp.dot(rows[...], weights[:, col], preferred_element_type=jnp.float32)
-            if total is not None:
-                product = (product + sums[:, col]).astype(jnp.bfloat16)
-            result[:, col] = product
-            target = out.at[:, col] if total is None else out.at[0, :, col]
+            result[:, col] = product.astype(jnp.bfloat16)
+            target = out.at[0, :, col]
             stores.append(pltpu.make_async_copy(result.at[:, col], target, sems.at[step]))
             stores[-1].start()
         for store in stores:
             store.wait()
 
-    kind = jnp.float32 if total is None else jnp.bfloat16
-    shape = (TILE, DOUT) if total is None else (1, TILE, DOUT)
+    shape = jax.ShapeDtypeStruct((1, TILE, DOUT), jnp.bfloat16)
     scratch = [
         pltpu.VMEM((TILE, deep), jnp.bfloat16),
         pltpu.VMEM((deep, DOUT), jnp.bfloat16),
-        pltpu.VMEM((TILE, DOUT), kind),
+        pltpu.VMEM((TILE, DOUT), jnp.bfloat16),
+        pltpu.SemaphoreType.DMA((RING * len(pieces) + RING,)),
     ]
-    if total is not None:
-        scratch.append(pltpu.VMEM((TILE, DOUT), jnp.float32))
-    scratch.append(pltpu.SemaphoreType.DMA((RING * len(pieces) + RING + 1,)))
     return call(
         kernel,
         f"project{first}",
-        jax.ShapeDtypeStruct(shape, kind),
+        shape,
         scratch,
         2 * TILE * deep * DOUT,
         8_000_000,
         0,
-    )(part, near, far, *([] if total is None else [total]))
+    )(part, near, far)
 
 
 def per_device(queries, key_rows, value_rows, tile_lists, tile_counts, out_weight):
@@ -325,16 +313,9 @@
     edges = halo(key_values)
     lists = query[:, TILE, :8].astype(jnp.int32)
     query, edges = lax.optimization_barrier((query, edges))
-    parts = []
-    for first, heads in CHUNKS:
-        mixed = attend(first, heads, lists, key_values, query, *edges)
-        if parts:
-            mixed, parts[-1] = lax.optimization_barrier((mixed, parts[-1]))
-        else:
-            mixed, query = lax.optimization_barrier((mixed, query))
-        parts.append(exchange(mixed))
-    total = project(*CHUNKS[0], parts[0], near, far)
-    return project(*CHUNKS[1], parts[1], near, far, total)
+    first, heads = CHUNKS[0]
+    mixed = attend(first, heads, lists, key_values, query, *edges)
+    return project(first, heads, exchange(mixed), near, far)
 
 
 def solution(mesh):

time: 135 us -> 131 us (0.970)
  blocking collectives: 21 us -> 38.8 us
  starting transfers between devices: 26.6 us -> 18.7 us
  waiting for transfers between devices: 34.9 us -> 28.3 us
  Pallas kernels: 30.4 us -> 24.2 us
    all_to_all x1 -> x2, blocking collectives: 21 us -> 38.8 us  [exchange(): return lax.all_to_all(value, 'ctx', 0, 0, axis_index_groups=groups)]
    all_to_all x3 -> x1, starting transfers between devices: 12.5 us -> 4.63 us  [exchange(): return lax.all_to_all(value, 'ctx', 0, 0, axis_index_groups=groups)]
    all_to_all x3 -> x1, waiting for transfers between devices: 6.58 us -> 0.01 us  [exchange(): return lax.all_to_all(value, 'ctx', 0, 0, axis_index_groups=groups)]
    pallas_call x6 -> x4, Pallas kernels: 30.4 us -> 24.2 us  [run(): pl.pallas_call(kernel, out_shape=outs, in_specs=specs, out_specs=jax.tree...]
  transfers between devices with their start and end apart: 8 -> 6, of which waited for: 5 -> 3; matrix products, arithmetic and copies ran while one was open for 2% -> 3% of each run, Pallas kernels for 18% -> 12%
where the time goes in v3:
time: 131 us; the launch traced here: 129 us
  blocking collectives  38.8 us (30%)
  waiting for transfers between devices  28.3 us (22%)
  Pallas kernels  24.2 us (18%)
  starting transfers between devices  18.7 us (14%)
  between operations  14.2 us (11%)
  local copies, waits for them, and re-layouts  3.75 us (3%)
  other arithmetic  1.33 us (1%)
    all_to_all x2, blocking collectives, exchange(): return lax.all_to_all(value, 'ctx', 0, 0, axis_index_groups=groups)  38.8 us
    pallas_call x4, Pallas kernels, run(): pl.pallas_call(kernel, out_shape=outs, in_specs=specs, out_specs=jax.tree...  24.2 us
    ppermute x1, waiting for transfers between devices, per_device(): other = lax.ppermute(out_weight, ('dp', 'ctx'), mirror_pairs())  21.9 us
    ppermute x1, starting transfers between devices, per_device(): other = lax.ppermute(out_weight, ('dp', 'ctx'), mirror_pairs())  11.4 us
    all_to_all x1, starting transfers between devices, exchange(): return lax.all_to_all(value, 'ctx', 0, 0, axis_index_groups=groups)  4.63 us
    ppermute x1, waiting for transfers between devices, halo(): lax.ppermute(value[:2], 'ctx', z_pairs(-1))  4.19 us
  transfers between devices with their start and end apart: 6, of which 3 were waited for; matrix products, arithmetic and copies ran while one was open for 3% of the time, Pallas kernels for 12%

profile of v3, /device:TPU:6, one launch (start us, length us, event | category | flops | bytes accessed | tf_op | source)
XLA Modules:
  0.0 129.3 jit_solution(2810838270727278519)
XLA Ops:
  6.5 0.0 all-gather.3.cloned.1.call-start
  6.5 2.6 %pack2.1 = bf16[4,768,384]{2,1,0:T(8,128)(2,1)} custom-call(bf16[1,384,1536]{2,1,0:T(8,128)(2,1)} %refs_0_.1, bf16[1,384,1536]{2,1,0:T(8,128)(2,1)} %refs_1_.1), custom_call_target="tpu_custom_call" | custom-call | bytes 4718592 | tf_op jit(solution)/shard_map/pack2/pallas_call | solution.py:54
  9.1 0.0 all-gather.3.cloned.1.call-update
  9.1 0.0 copy-start.2
  9.1 0.0 copy-start.6
  9.2 4.6 %all-to-all-start = ((bf16[4,768,384]{2,1,0:T(8,128)(2,1)}), bf16[4,768,384]{2,1,0:T(8,128)(2,1)}, u32[]{:S(2)}, u32[]{:S(2)}) async-start(bf16[4,768,384]{2,1,0:T(8,128)(2,1)} %pack2.1), calls=%async_computation | async-start | bytes 4718592 | tf_op jit(solution)/shard_map/all_to_all | solution.py:285
  13.8 0.0 all-gather.5.cloned.1.call-start
  13.8 0.0 copy-done.2
  13.9 11.4 %collective-permute-start = (bf16[96,1536]{1,0:T(8,128)(2,1)S(1)}, bf16[96,1536]{1,0:T(8,128)(2,1)S(1)}, u32[]{:S(2)}, u32[]{:S(2)}) collective-permute-start(bf16[96,1536]{1,0:T(8,128)(2,1)S(1)} %copy-done.2), channel_id=1, source_target_pairs={{0,92},{1,93},{2,94},{3,95},{4,88},{5,89},{6,90},{7,91},{8,84},{9,... | collective-permute-start | bytes 884744 | tf_op jit(solution)/shard_map/ppermute | solution.py:306
  25.9 0.0 copy-done.6
  25.9 0.7 fusion.5.refs_1_
  26.6 2.7 %pack1.1 = bf16[4,400,384]{2,1,0:T(8,128)(2,1)} custom-call(bf16[1,384,1536]{2,1,0:T(8,128)(2,1)} %refs_0_.2, bf16[16,384]{1,0:T(8,128)(2,1)} %fusion.5.refs_1_), custom_call_target="tpu_custom_call" | custom-call | bytes 2457600 | tf_op jit(solution)/shard_map/pack1/pallas_call | solution.py:54
  29.3 21.9 %collective-permute-done = bf16[96,1536]{1,0:T(8,128)(2,1)S(1)} collective-permute-done((bf16[96,1536]{1,0:T(8,128)(2,1)S(1)}, bf16[96,1536]{1,0:T(8,128)(2,1)S(1)}, u32[]{:S(2)}, u32[]{:S(2)}) %collective-permute-start) | collective-permute-done | bytes 294944 | tf_op jit(solution)/shard_map/ppermute | solution.py:306
  51.2 0.0 copy-start.3
  51.2 0.0 all-to-all-done.refs_1_
  51.2 0.7 copy-done.3
  51.9 0.0 all-gather.5.cloned.1.call-update
  52.0 0.0 copy-start
  52.0 2.0 %fusion.6 = (bf16[2,768,384]{2,1,0:T(8,128)(2,1)S(1)}, bf16[2,768,384]{2,1,0:T(8,128)(2,1)S(1)}) fusion(bf16[4,768,384]{2,1,0:T(8,128)(2,1)} %all-to-all-done.refs_1_), kind=kLoop, calls=%fused_computation.10 | loop fusion | bytes 4718592 | tf_op jit(solution)/shard_map/slice | solution.py:293
  53.9 1.4 %collective-permute-start.1 = (bf16[2,768,384]{2,1,0:T(8,128)(2,1)S(1)}, bf16[2,768,384]{2,1,0:T(8,128)(2,1)S(1)}, u32[]{:S(2)}, u32[]{:S(2)}) collective-permute-start(bf16[2,768,384]{2,1,0:T(8,128)(2,1)S(1)} %get-tuple-element.26), channel_id=1, source_target_pairs={{0,4},{1,5},{2,6},{3,7},{4,8},{5,9},{6,10},{7,11},{8,12},{9,13},{1... | collective-permute-start | bytes 3538952 | tf_op jit(solution)/shard_map/ppermute | solution.py:292
  55.3 1.3 collective-permute-start.2
  56.6 0.0 copy-done
  56.6 21.0 %all_to_all.15.refs_2_ = bf16[4,400,384]{2,1,0:T(8,128)(2,1)S(1)} all-to-all(bf16[4,400,384]{2,1,0:T(8,128)(2,1)S(1)} %copy-done), channel_id=1, replica_groups={{0,1,2,3},{4,5,6,7},{8,9,10,11},{12,13,14,15},{16,17,18,19},{20,21,22,2..., dimensions={0} | all-to-all | bytes 2457600 | tf_op jit(solution)/shard_map/all_to_all | solution.py:285
  77.7 0.0 copy-start.1
  77.7 0.7 slice_convert_fusion
  78.3 2.2 %collective-permute-done.1.refs_3_ = bf16[2,768,384]{2,1,0:T(8,128)(2,1)S(1)} collective-permute-done((bf16[2,768,384]{2,1,0:T(8,128)(2,1)S(1)}, bf16[2,768,384]{2,1,0:T(8,128)(2,1)S(1)}, u32[]{:S(2)}, u32[]{:S(2)}) %collective-permute-start.1) | collective-permute-done | bytes 1179680 | tf_op jit(solution)/shard_map/ppermute | solution.py:292
  80.5 0.0 copy-start.4
  80.5 4.2 %collective-permute-done.2.refs_4_ = bf16[2,768,384]{2,1,0:T(8,128)(2,1)S(1)} collective-permute-done((bf16[2,768,384]{2,1,0:T(8,128)(2,1)S(1)}, bf16[2,768,384]{2,1,0:T(8,128)(2,1)S(1)}, u32[]{:S(2)}, u32[]{:S(2)}) %collective-permute-start.2) | collective-permute-done | bytes 1179680 | tf_op jit(solution)/shard_map/ppermute | solution.py:293
  84.7 0.0 copy-done.4
  84.7 0.0 copy-start.5
  84.7 1.0 copy-done.5
  85.7 0.0 copy-done.1
  85.7 13.4 %attend0.1 = bf16[4,384,384]{2,1,0:T(8,128)(2,1)} custom-call(s32[4,8]{1,0:T(4,128)} %bitcast.3, bf16[4,768,384]{2,1,0:T(8,128)(2,1)} %all-to-all-done.refs_1_, bf16[4,400,384]{2,1,0:T(8,128)(2,1)} %copy-done.1, bf16[2,768,384]{2,1,0:T(8,128)(2,1)} %copy-done.4, bf16[2,768,384]{2,1,0:T(8,128)(2,1)} %copy-done.5), custom_call_target="tpu_custom_call" | custom-call | flops 15000000512 | bytes 4800000 | tf_op jit(solution)/shard_map/attend0/pallas_call | solution.py:54
  99.1 17.7 %all_to_all.16.refs_0_ = bf16[4,384,384]{2,1,0:T(8,128)(2,1)} all-to-all(bf16[4,384,384]{2,1,0:T(8,128)(2,1)} %attend0.1), channel_id=1, replica_groups={{0,1,2,3},{4,5,6,7},{8,9,10,11},{12,13,14,15},{16,17,18,19},{20,21,22,2..., dimensions={0} | all-to-all | bytes 2359296 | tf_op jit(solution)/shard_map/all_to_all | solution.py:285
  116.8 0.0 all-gather.3.cloned.1.call-done.refs_1_
  116.8 0.0 all-gather.5.cloned.1.call-done.refs_2_
  116.8 5.6 %project0.1 = bf16[1,384,1536]{2,1,0:T(8,128)(2,1)} custom-call(bf16[4,384,384]{2,1,0:T(8,128)(2,1)} %all_to_all.16.refs_0_, bf16[768,1536]{1,0:T(8,128)(2,1)} %all-gather.3.cloned.1.call-done.refs_1_, bf16[768,1536]{1,0:T(8,128)(2,1)} %all-gather.5.cloned.1.call-done.refs_2_), custom_call_target="tpu_custom_call" | custom-call | flops 1811939328 | bytes 8000000 | tf_op jit(solution)/shard_map/project0/pallas_call | solution.py:54
  (1 shorter events, 0.0 us)
Async XLA Ops:
  6.5 110.3 %all-gather.3.cloned.1.call-start = ((), (), s32[]{:S(2)}) async-start(), calls=%async_computation.3 | async-start | bytes 2654208 | tf_op jit(solution)/shard_map/all_gather | solution.py:288
  9.1 4.7 %copy-start.2 = (bf16[96,1536]{1,0:T(8,128)(2,1)S(1)}, bf16[96,1536]{1,0:T(8,128)(2,1)}, u32[]{:S(2)}) copy-start(bf16[96,1536]{1,0:T(8,128)(2,1)} %param.11) | copy-start | bytes 884740
  9.1 16.8 %copy-start.6 = (s32[1,1,5]{2,1,0:T(1,128)S(1)}, s32[1,1,5]{2,1,0:T(1,128)}, u32[]{:S(2)}) copy-start(s32[1,1,5]{2,1,0:T(1,128)} %param.9) | copy-start | bytes 64
  9.2 42.1 %all-to-all-start = ((bf16[4,768,384]{2,1,0:T(8,128)(2,1)}), bf16[4,768,384]{2,1,0:T(8,128)(2,1)}, u32[]{:S(2)}, u32[]{:S(2)}) async-start(bf16[4,768,384]{2,1,0:T(8,128)(2,1)} %pack2.1), calls=%async_computation | async-start | bytes 4718592 | tf_op jit(solution)/shard_map/all_to_all | solution.py:285
  13.8 103.0 %all-gather.5.cloned.1.call-start = ((), (), s32[]{:S(2)}) async-start(), calls=%async_computation.4 | async-start | bytes 2654208 | tf_op jit(solution)/shard_map/all_gather | solution.py:288
  13.9 37.4 %collective-permute-start = (bf16[96,1536]{1,0:T(8,128)(2,1)S(1)}, bf16[96,1536]{1,0:T(8,128)(2,1)S(1)}, u32[]{:S(2)}, u32[]{:S(2)}) collective-permute-start(bf16[96,1536]{1,0:T(8,128)(2,1)S(1)} %copy-done.2), channel_id=1, source_target_pairs={{0,92},{1,93},{2,94},{3,95},{4,88},{5,89},{6,90},{7,91},{8,84},{9,... | collective-permute-start | bytes 884744 | tf_op jit(solution)/shard_map/ppermute | solution.py:306
  51.2 0.7 copy-start.3
  52.0 4.6 %copy-start = (bf16[4,400,384]{2,1,0:T(8,128)(2,1)S(1)}, bf16[4,400,384]{2,1,0:T(8,128)(2,1)}, u32[]{:S(2)}) copy-start(bf16[4,400,384]{2,1,0:T(8,128)(2,1)} %pack1.1) | copy-start | bytes 3686404
  53.9 26.5 %collective-permute-start.1 = (bf16[2,768,384]{2,1,0:T(8,128)(2,1)S(1)}, bf16[2,768,384]{2,1,0:T(8,128)(2,1)S(1)}, u32[]{:S(2)}, u32[]{:S(2)}) collective-permute-start(bf16[2,768,384]{2,1,0:T(8,128)(2,1)S(1)} %get-tuple-element.26), channel_id=1, source_target_pairs={{0,4},{1,5},{2,6},{3,7},{4,8},{5,9},{6,10},{7,11},{8,12},{9,13},{1... | collective-permute-start | bytes 3538952 | tf_op jit(solution)/shard_map/ppermute | solution.py:292
  55.3 29.4 %collective-permute-start.2 = (bf16[2,768,384]{2,1,0:T(8,128)(2,1)S(1)}, bf16[2,768,384]{2,1,0:T(8,128)(2,1)S(1)}, u32[]{:S(2)}, u32[]{:S(2)}) collective-permute-start(bf16[2,768,384]{2,1,0:T(8,128)(2,1)S(1)} %get-tuple-element.25), channel_id=1, source_target_pairs={{4,0},{5,1},{6,2},{7,3},{8,4},{9,5},{10,6},{11,7},{12,8},{13,9},{1... | collective-permute-start | bytes 3538952 | tf_op jit(solution)/shard_map/ppermute | solution.py:293
  77.7 8.1 %copy-start.1 = (bf16[4,400,384]{2,1,0:T(8,128)(2,1)}, bf16[4,400,384]{2,1,0:T(8,128)(2,1)S(1)}, u32[]{:S(2)}) copy-start(bf16[4,400,384]{2,1,0:T(8,128)(2,1)S(1)} %all_to_all.15.refs_2_) | copy-start | bytes 3686404
  80.5 4.2 %copy-start.4 = (bf16[2,768,384]{2,1,0:T(8,128)(2,1)}, bf16[2,768,384]{2,1,0:T(8,128)(2,1)S(1)}, u32[]{:S(2)}) copy-start(bf16[2,768,384]{2,1,0:T(8,128)(2,1)S(1)} %collective-permute-done.1.refs_3_) | copy-start | bytes 3538948
  84.7 1.0 copy-start.5
Sparse Core Ops, SparseCore 0:
  9.5 36.6 all-gather.2
  52.1 30.0 all-gather.4

commit v4 on v3

--- a/solution.py
+++ b/solution.py
@@ -220,18 +220,29 @@
 
         def weight_copies(own):
             copies = []
-            for g in range(RING):
-                for to, count, core, half, at in pieces:
-                    source = near_in if half == own else far_in
-                    copies.append(
-                        pltpu.make_async_copy(
-                            source.at[pl.ds((2 * g + core) * 96 + at, count)],
-                            weights.at[pl.ds(g * wide + to, count)],
-                            sems.at[len(copies)],
+            for step in range(DOUT // 512):
+                col = pl.ds(step * 512, 512)
+                for g in range(RING):
+                    for to, count, core, half, at in pieces:
+                        source = near_in if half == own else far_in
+                        copies.append(
+                            pltpu.make_async_copy(
+                                source.at[pl.ds((2 * g + core) * 96 + at, count), col],
+                                weights.at[pl.ds(g * wide + to, count), col],
+                                sems.at[len(copies)],
+                            )
                         )
-                    )
             return copies
 
+        waits = weight_copies(0)
+        each = RING * len(pieces)
+        parts = []
+        for g in range(RING):
+            copy = pltpu.make_async_copy(
+                part_in.at[g], rows.at[:, pl.ds(g * wide, wide)], sems.at[len(waits) + g]
+            )
+            copy.start()
+            parts.append(copy)
         for own in range(2):
 
             @pl.when(z_half == own)
@@ -239,22 +250,17 @@
                 for copy in weight_copies(own):
                     copy.start()
 
-        waits = weight_copies(0)
-        for g in range(RING):
-            copy = pltpu.make_async_copy(
-                part_in.at[g], rows.at[:, pl.ds(g * wide, wide)], sems.at[len(waits)]
-            )
-            copy.start()
-            waits.append(copy)
-        for copy in waits:
+        for copy in parts:
             copy.wait()
         stores = []
         for step in range(DOUT // 512):
+            for copy in waits[step * each : (step + 1) * each]:
+                copy.wait()
             col = pl.ds(step * 512, 512)
             product = jnp.dot(rows[...], weights[:, col], preferred_element_type=jnp.float32)
             result[:, col] = product.astype(jnp.bfloat16)
             target = out.at[0, :, col]
-            stores.append(pltpu.make_async_copy(result.at[:, col], target, sems.at[step]))
+            stores.append(pltpu.make_async_copy(result.at[:, col], target, sems.at[len(waits) + step]))
             stores[-1].start()
         for store in stores:
             store.wait()
@@ -264,7 +270,7 @@
         pltpu.VMEM((TILE, deep), jnp.bfloat16),
         pltpu.VMEM((deep, DOUT), jnp.bfloat16),
         pltpu.VMEM((TILE, DOUT), jnp.bfloat16),
-        pltpu.SemaphoreType.DMA((RING * len(pieces) + RING,)),
+        pltpu.SemaphoreType.DMA((DOUT // 512 * RING * len(pieces) + RING,)),
     ]
     return call(
         kernel,

time: 131 us -> 132 us (level)
  blocking collectives: 38.8 us -> 40.5 us
    all_to_all x2, blocking collectives: 38.8 us -> 40.5 us  [exchange(): return lax.all_to_all(value, 'ctx', 0, 0, axis_index_groups=groups)]
where the time goes in v4:
time: 132 us; the launch traced here: 130 us
  blocking collectives  40.5 us (31%)
  waiting for transfers between devices  28.3 us (21%)
  Pallas kernels  23.1 us (18%)
  starting transfers between devices  18.7 us (14%)
  between operations  14.2 us (11%)
  local copies, waits for them, and re-layouts  3.75 us (3%)
  other arithmetic  1.33 us (1%)
    all_to_all x2, blocking collectives, exchange(): return lax.all_to_all(value, 'ctx', 0, 0, axis_index_groups=groups)  40.5 us
    pallas_call x4, Pallas kernels, run(): pl.pallas_call(kernel, out_shape=outs, in_specs=specs, out_specs=jax.tree...  23.1 us
    ppermute x1, waiting for transfers between devices, per_device(): other = lax.ppermute(out_weight, ('dp', 'ctx'), mirror_pairs())  21.9 us
    ppermute x1, starting transfers between devices, per_device(): other = lax.ppermute(out_weight, ('dp', 'ctx'), mirror_pairs())  11.4 us
    all_to_all x1, starting transfers between devices, exchange(): return lax.all_to_all(value, 'ctx', 0, 0, axis_index_groups=groups)  4.63 us
    ppermute x1, waiting for transfers between devices, halo(): lax.ppermute(value[:2], 'ctx', z_pairs(-1))  4.19 us
  transfers between devices with their start and end apart: 6, of which 3 were waited for; matrix products, arithmetic and copies ran while one was open for 3% of the time, Pallas kernels for 12%

profile of v4, /device:TPU:6, one launch (start us, length us, event | category | flops | bytes accessed | tf_op | source)
XLA Modules:
  0.0 130.0 jit_solution(3736898749765697210)
XLA Ops:
  6.5 0.0 all-gather.3.cloned.1.call-start
  6.5 2.6 %pack2.1 = bf16[4,768,384]{2,1,0:T(8,128)(2,1)} custom-call(bf16[1,384,1536]{2,1,0:T(8,128)(2,1)} %refs_0_.1, bf16[1,384,1536]{2,1,0:T(8,128)(2,1)} %refs_1_.1), custom_call_target="tpu_custom_call" | custom-call | bytes 4718592 | tf_op jit(solution)/shard_map/pack2/pallas_call | solution.py:54
  9.1 0.0 all-gather.3.cloned.1.call-update
  9.1 0.0 copy-start.2
  9.1 0.0 copy-start.6
  9.2 4.6 %all-to-all-start = ((bf16[4,768,384]{2,1,0:T(8,128)(2,1)}), bf16[4,768,384]{2,1,0:T(8,128)(2,1)}, u32[]{:S(2)}, u32[]{:S(2)}) async-start(bf16[4,768,384]{2,1,0:T(8,128)(2,1)} %pack2.1), calls=%async_computation | async-start | bytes 4718592 | tf_op jit(solution)/shard_map/all_to_all | solution.py:291
  13.8 0.0 all-gather.5.cloned.1.call-start
  13.8 0.0 copy-done.2
  13.9 11.4 %collective-permute-start = (bf16[96,1536]{1,0:T(8,128)(2,1)S(1)}, bf16[96,1536]{1,0:T(8,128)(2,1)S(1)}, u32[]{:S(2)}, u32[]{:S(2)}) collective-permute-start(bf16[96,1536]{1,0:T(8,128)(2,1)S(1)} %copy-done.2), channel_id=1, source_target_pairs={{0,92},{1,93},{2,94},{3,95},{4,88},{5,89},{6,90},{7,91},{8,84},{9,... | collective-permute-start | bytes 884744 | tf_op jit(solution)/shard_map/ppermute | solution.py:312
  25.9 0.0 copy-done.6
  25.9 0.7 fusion.5.refs_1_
  26.6 2.7 %pack1.1 = bf16[4,400,384]{2,1,0:T(8,128)(2,1)} custom-call(bf16[1,384,1536]{2,1,0:T(8,128)(2,1)} %refs_0_.2, bf16[16,384]{1,0:T(8,128)(2,1)} %fusion.5.refs_1_), custom_call_target="tpu_custom_call" | custom-call | bytes 2457600 | tf_op jit(solution)/shard_map/pack1/pallas_call | solution.py:54
  29.3 21.9 %collective-permute-done = bf16[96,1536]{1,0:T(8,128)(2,1)S(1)} collective-permute-done((bf16[96,1536]{1,0:T(8,128)(2,1)S(1)}, bf16[96,1536]{1,0:T(8,128)(2,1)S(1)}, u32[]{:S(2)}, u32[]{:S(2)}) %collective-permute-start) | collective-permute-done | bytes 294944 | tf_op jit(solution)/shard_map/ppermute | solution.py:312
  51.2 0.0 copy-start.3
  51.2 0.0 all-to-all-done.refs_1_
  51.2 0.7 copy-done.3
  51.9 0.0 all-gather.5.cloned.1.call-update
  52.0 0.0 copy-start
  52.0 2.0 %fusion.6 = (bf16[2,768,384]{2,1,0:T(8,128)(2,1)S(1)}, bf16[2,768,384]{2,1,0:T(8,128)(2,1)S(1)}) fusion(bf16[4,768,384]{2,1,0:T(8,128)(2,1)} %all-to-all-done.refs_1_), kind=kLoop, calls=%fused_computation.10 | loop fusion | bytes 4718592 | tf_op jit(solution)/shard_map/slice | solution.py:299
  53.9 1.4 %collective-permute-start.1 = (bf16[2,768,384]{2,1,0:T(8,128)(2,1)S(1)}, bf16[2,768,384]{2,1,0:T(8,128)(2,1)S(1)}, u32[]{:S(2)}, u32[]{:S(2)}) collective-permute-start(bf16[2,768,384]{2,1,0:T(8,128)(2,1)S(1)} %get-tuple-element.26), channel_id=1, source_target_pairs={{0,4},{1,5},{2,6},{3,7},{4,8},{5,9},{6,10},{7,11},{8,12},{9,13},{1... | collective-permute-start | bytes 3538952 | tf_op jit(solution)/shard_map/ppermute | solution.py:298
  55.3 1.3 collective-permute-start.2
  56.6 0.0 copy-done
  56.6 21.0 %all_to_all.15.refs_2_ = bf16[4,400,384]{2,1,0:T(8,128)(2,1)S(1)} all-to-all(bf16[4,400,384]{2,1,0:T(8,128)(2,1)S(1)} %copy-done), channel_id=1, replica_groups={{0,1,2,3},{4,5,6,7},{8,9,10,11},{12,13,14,15},{16,17,18,19},{20,21,22,2..., dimensions={0} | all-to-all | bytes 2457600 | tf_op jit(solution)/shard_map/all_to_all | solution.py:291
  77.7 0.0 copy-start.1
  77.7 0.7 slice_convert_fusion
  78.3 2.2 %collective-permute-done.1.refs_3_ = bf16[2,768,384]{2,1,0:T(8,128)(2,1)S(1)} collective-permute-done((bf16[2,768,384]{2,1,0:T(8,128)(2,1)S(1)}, bf16[2,768,384]{2,1,0:T(8,128)(2,1)S(1)}, u32[]{:S(2)}, u32[]{:S(2)}) %collective-permute-start.1) | collective-permute-done | bytes 1179680 | tf_op jit(solution)/shard_map/ppermute | solution.py:298
  80.5 0.0 copy-start.4
  80.5 4.2 %collective-permute-done.2.refs_4_ = bf16[2,768,384]{2,1,0:T(8,128)(2,1)S(1)} collective-permute-done((bf16[2,768,384]{2,1,0:T(8,128)(2,1)S(1)}, bf16[2,768,384]{2,1,0:T(8,128)(2,1)S(1)}, u32[]{:S(2)}, u32[]{:S(2)}) %collective-permute-start.2) | collective-permute-done | bytes 1179680 | tf_op jit(solution)/shard_map/ppermute | solution.py:299
  84.7 0.0 copy-done.4
  84.7 0.0 copy-start.5
  84.7 1.0 copy-done.5
  85.7 0.0 copy-done.1
  85.7 12.6 %attend0.1 = bf16[4,384,384]{2,1,0:T(8,128)(2,1)} custom-call(s32[4,8]{1,0:T(4,128)} %bitcast.3, bf16[4,768,384]{2,1,0:T(8,128)(2,1)} %all-to-all-done.refs_1_, bf16[4,400,384]{2,1,0:T(8,128)(2,1)} %copy-done.1, bf16[2,768,384]{2,1,0:T(8,128)(2,1)} %copy-done.4, bf16[2,768,384]{2,1,0:T(8,128)(2,1)} %copy-done.5), custom_call_target="tpu_custom_call" | custom-call | flops 15000000512 | bytes 4800000 | tf_op jit(solution)/shard_map/attend0/pallas_call | solution.py:54
  98.3 19.5 %all_to_all.16.refs_0_ = bf16[4,384,384]{2,1,0:T(8,128)(2,1)} all-to-all(bf16[4,384,384]{2,1,0:T(8,128)(2,1)} %attend0.1), channel_id=1, replica_groups={{0,1,2,3},{4,5,6,7},{8,9,10,11},{12,13,14,15},{16,17,18,19},{20,21,22,2..., dimensions={0} | all-to-all | bytes 2359296 | tf_op jit(solution)/shard_map/all_to_all | solution.py:291
  117.8 0.0 all-gather.3.cloned.1.call-done.refs_1_
  117.8 0.0 all-gather.5.cloned.1.call-done.refs_2_
  117.8 5.3 %project0.1 = bf16[1,384,1536]{2,1,0:T(8,128)(2,1)} custom-call(bf16[4,384,384]{2,1,0:T(8,128)(2,1)} %all_to_all.16.refs_0_, bf16[768,1536]{1,0:T(8,128)(2,1)} %all-gather.3.cloned.1.call-done.refs_1_, bf16[768,1536]{1,0:T(8,128)(2,1)} %all-gather.5.cloned.1.call-done.refs_2_), custom_call_target="tpu_custom_call" | custom-call | flops 1811939328 | bytes 8000000 | tf_op jit(solution)/shard_map/project0/pallas_call | solution.py:54
  (1 shorter events, 0.0 us)
Async XLA Ops:
  6.5 111.3 %all-gather.3.cloned.1.call-start = ((), (), s32[]{:S(2)}) async-start(), calls=%async_computation.3 | async-start | bytes 2654208 | tf_op jit(solution)/shard_map/all_gather | solution.py:294
  9.1 4.7 %copy-start.2 = (bf16[96,1536]{1,0:T(8,128)(2,1)S(1)}, bf16[96,1536]{1,0:T(8,128)(2,1)}, u32[]{:S(2)}) copy-start(bf16[96,1536]{1,0:T(8,128)(2,1)} %param.11) | copy-start | bytes 884740
  9.1 16.8 %copy-start.6 = (s32[1,1,5]{2,1,0:T(1,128)S(1)}, s32[1,1,5]{2,1,0:T(1,128)}, u32[]{:S(2)}) copy-start(s32[1,1,5]{2,1,0:T(1,128)} %param.9) | copy-start | bytes 64
  9.2 42.1 %all-to-all-start = ((bf16[4,768,384]{2,1,0:T(8,128)(2,1)}), bf16[4,768,384]{2,1,0:T(8,128)(2,1)}, u32[]{:S(2)}, u32[]{:S(2)}) async-start(bf16[4,768,384]{2,1,0:T(8,128)(2,1)} %pack2.1), calls=%async_computation | async-start | bytes 4718592 | tf_op jit(solution)/shard_map/all_to_all | solution.py:291
  13.8 104.0 %all-gather.5.cloned.1.call-start = ((), (), s32[]{:S(2)}) async-start(), calls=%async_computation.4 | async-start | bytes 2654208 | tf_op jit(solution)/shard_map/all_gather | solution.py:294
  13.9 37.4 %collective-permute-start = (bf16[96,1536]{1,0:T(8,128)(2,1)S(1)}, bf16[96,1536]{1,0:T(8,128)(2,1)S(1)}, u32[]{:S(2)}, u32[]{:S(2)}) collective-permute-start(bf16[96,1536]{1,0:T(8,128)(2,1)S(1)} %copy-done.2), channel_id=1, source_target_pairs={{0,92},{1,93},{2,94},{3,95},{4,88},{5,89},{6,90},{7,91},{8,84},{9,... | collective-permute-start | bytes 884744 | tf_op jit(solution)/shard_map/ppermute | solution.py:312
  51.2 0.7 copy-start.3
  52.0 4.6 %copy-start = (bf16[4,400,384]{2,1,0:T(8,128)(2,1)S(1)}, bf16[4,400,384]{2,1,0:T(8,128)(2,1)}, u32[]{:S(2)}) copy-start(bf16[4,400,384]{2,1,0:T(8,128)(2,1)} %pack1.1) | copy-start | bytes 3686404
  53.9 26.5 %collective-permute-start.1 = (bf16[2,768,384]{2,1,0:T(8,128)(2,1)S(1)}, bf16[2,768,384]{2,1,0:T(8,128)(2,1)S(1)}, u32[]{:S(2)}, u32[]{:S(2)}) collective-permute-start(bf16[2,768,384]{2,1,0:T(8,128)(2,1)S(1)} %get-tuple-element.26), channel_id=1, source_target_pairs={{0,4},{1,5},{2,6},{3,7},{4,8},{5,9},{6,10},{7,11},{8,12},{9,13},{1... | collective-permute-start | bytes 3538952 | tf_op jit(solution)/shard_map/ppermute | solution.py:298
  55.3 29.4 %collective-permute-start.2 = (bf16[2,768,384]{2,1,0:T(8,128)(2,1)S(1)}, bf16[2,768,384]{2,1,0:T(8,128)(2,1)S(1)}, u32[]{:S(2)}, u32[]{:S(2)}) collective-permute-start(bf16[2,768,384]{2,1,0:T(8,128)(2,1)S(1)} %get-tuple-element.25), channel_id=1, source_target_pairs={{4,0},{5,1},{6,2},{7,3},{8,4},{9,5},{10,6},{11,7},{12,8},{13,9},{1... | collective-permute-start | bytes 3538952 | tf_op jit(solution)/shard_map/ppermute | solution.py:299
  77.7 8.1 %copy-start.1 = (bf16[4,400,384]{2,1,0:T(8,128)(2,1)}, bf16[4,400,384]{2,1,0:T(8,128)(2,1)S(1)}, u32[]{:S(2)}) copy-start(bf16[4,400,384]{2,1,0:T(8,128)(2,1)S(1)} %all_to_all.15.refs_2_) | copy-start | bytes 3686404
  80.5 4.2 %copy-start.4 = (bf16[2,768,384]{2,1,0:T(8,128)(2,1)}, bf16[2,768,384]{2,1,0:T(8,128)(2,1)S(1)}, u32[]{:S(2)}) copy-start(bf16[2,768,384]{2,1,0:T(8,128)(2,1)S(1)} %collective-permute-done.1.refs_3_) | copy-start | bytes 3538948
  84.7 1.0 copy-start.5
Sparse Core Ops, SparseCore 0:
  9.5 36.6 all-gather.2
  52.1 30.0 all-gather.4
